TPU v7x, 512 devices: a whole 4x8x8 slice. The times are simulated.
512 devices in a mesh: depth: 32 (over z_hi, x, core), plan: 16 (over y, z_lo).
Axes of the slice: x: 4, y: 8, z: 8 (z_hi: 4, z_lo: 2; z = z_hi * 2 + z_lo), core: 2. Of those that a mesh axis runs over, the one named last changes fastest.
Arguments:
- stress: float32 [6, 256, 256, 256], P(None, 'depth', 'plan'), may hold values from -6 to 6
- velocity: float32 [3, 256, 256, 256], P(None, 'depth', 'plan'), may hold values from -3 to 3
- density: float32 [256, 256, 256], P('depth', 'plan'), may hold values from 1 to 4
- branch_flags: int32 [256, 256, 256], P('depth', 'plan'), may hold values from 0 to 2
- pile_velocity: float32 [3, 196608], P(None, 'depth'), may hold values from -3 to 3
- pile_mass: float32 [196608], P('depth'), may hold values from 0.5 to 2
- jack_force: float32 [3, 196608], P(None, 'depth'), may hold values from -6 to 6
- pair_elem: int32 [32, 32768], P('depth', 'plan'), may hold values from 0 to 18431, as said below
- pair_cell: int32 [32, 32768], P('depth', 'plan'), may hold values from -1 to 32767, as said below
Outputs:
- stress_out: float32 [6, 256, 256, 256], P(None, 'depth', 'plan')
- velocity_out: float32 [3, 256, 256, 256], P(None, 'depth', 'plan')
- pile_velocity_out: float32 [3, 196608], P(None, 'depth')
Inputs may be any that keep to these rules, and one draw needn't show every extreme that they name: `pair_elem`: counted from block d - 1 for depth index d, it names an element of the pile: blocks d - 1, d, d + 1 only, never below block 0 or above the last block. `pair_cell`: live pairs (cell >= 0) of one device are its first slots; at most 2048 on one device; all slots live on every device of one depth index, the tip, which lies above the middle depth index and below the last; fewer live on the depth indices before it, none after it.
All inputs are finite; a program needn't handle non-finite values.
Results may differ from a plain program's by a relative error of at most 0.00016.
Values sent between devices are 32-bit elements; how exact they have to be, the bound alone decides.
A program may use at most 64 MiB of HBM per device.

v0:
```python
import math

import jax
import jax.numpy as jnp
from jax import lax
from jax.sharding import PartitionSpec as P

STEPS = 3


time_step = 0.2
penalty = 1.0
lame_first = 1.0
shear_modulus = 1.0
cone_rate = 1.5
symmetric_index = ((0, 3, 4), (3, 1, 5), (4, 5, 2))


def extended(shard, sides, width):
    edges = {}
    for axis, dim in sides:
        peers, length = (lax.axis_size(axis), shard.shape[dim])
        up = [(i, (i + 1) % peers) for i in range(peers - 1)]
        last = lax.slice_in_dim(shard, length - width, length, axis=dim)
        leading = lax.slice_in_dim(shard, 0, width, axis=dim)
        edges[dim] = (
            lax.ppermute(last, axis, up),
            lax.ppermute(leading, axis, [(b, a) for a, b in up]),
        )
    done = []
    for _, dim in sides:
        low, high = edges[dim]
        around = [(width, width) if d in done else (0, 0) for d in range(shard.ndim)]
        shard = jnp.concatenate([jnp.pad(low, around), shard, jnp.pad(high, around)], axis=dim)
        done.append(dim)
    return shard


def extended_2(block, sides, width):
    for axis, dim in sides:
        count = lax.axis_size(axis)
        forward = [(i, i + 1) for i in range(count - 1)]
        backward = [(target, source) for source, target in forward]
        low = lax.ppermute(
            lax.slice_in_dim(block, block.shape[dim] - width, None, axis=dim), axis, forward
        )
        high = lax.ppermute(lax.slice_in_dim(block, 0, width, axis=dim), axis, backward)
        block = jnp.concatenate([low, block, high], axis=dim)
    return block


def split_up(shard, dim, peers):
    before, after = (shard.shape[:dim], shard.shape[dim + 1 :])
    return jnp.moveaxis(shard.reshape(*before, peers, -1, *after), dim, 0)


def sent_and_summed(shard, axis, dim):
    parts = split_up(shard, dim, lax.axis_size(axis))
    arrived = lax.all_to_all(parts, axis, split_axis=0, concat_axis=0, tiled=True)
    return arrived.sum(axis=0)


def from_everyone(shard, axis):
    peers = lax.axis_size(axis)
    return lax.all_to_all(
        jnp.broadcast_to(shard[None], (peers, *shard.shape)), axis, 0, 0, tiled=True
    )


def joined_along(parts, dim):
    shape = list(parts.shape[1:])
    shape[dim] *= parts.shape[0]
    return jnp.moveaxis(parts, 0, dim).reshape(shape)


def gather_directly(shard, axis, dim):
    parts = from_everyone(shard, axis)
    return joined_along(parts, dim)


def slopes_of(padded):
    along_depth = 0.5 * (padded[:, 2:, 1:-1, 1:-1] - padded[:, :-2, 1:-1, 1:-1])
    along_plan = 0.5 * (padded[:, 1:-1, 2:, 1:-1] - padded[:, 1:-1, :-2, 1:-1])
    along_last = 0.5 * (padded[:, 1:-1, 1:-1, 2:] - padded[:, 1:-1, 1:-1, :-2])
    return (along_depth, along_plan, along_last)


def divergence(padded):
    slopes = slopes_of(padded)
    return jnp.stack(
        [
            slopes[0][symmetric_index[component][0]]
            + slopes[1][symmetric_index[component][1]]
            + slopes[2][symmetric_index[component][2]]
            for component in range(3)
        ]
    )


def strain_rate(padded):
    slopes = slopes_of(padded)
    return jnp.stack(
        [
            slopes[0][0],
            slopes[1][1],
            slopes[2][2],
            0.5 * (slopes[1][0] + slopes[0][1]),
            0.5 * (slopes[2][0] + slopes[0][2]),
            0.5 * (slopes[2][1] + slopes[1][2]),
        ]
    )


def return_map(trial_stress, branch_flags):
    pressure = (trial_stress[0] + trial_stress[1] + trial_stress[2]) / 3.0
    deviator = jnp.stack(
        [
            trial_stress[0] - pressure,
            trial_stress[1] - pressure,
            trial_stress[2] - pressure,
            trial_stress[3],
            trial_stress[4],
            trial_stress[5],
        ]
    )
    second = (
        0.5 * (deviator[0] * deviator[0] + deviator[1] * deviator[1] + deviator[2] * deviator[2])
        + deviator[3] * deviator[3]
        + deviator[4] * deviator[4]
        + deviator[5] * deviator[5]
    )
    shrink = 1.0 / (1.0 + cone_rate * jnp.sqrt(second))
    empty_part = jnp.zeros_like(pressure)
    spherical = jnp.stack([pressure, pressure, pressure, empty_part, empty_part, empty_part])
    cone_stress = deviator * shrink + spherical
    return jnp.where(
        branch_flags == 0, trial_stress, jnp.where(branch_flags == 1, cone_stress, spherical)
    )


def stress_update(stress, padded_velocity, branch_flags):
    strain = strain_rate(padded_velocity)
    increment = 2.0 * shear_modulus * strain
    increment = increment.at[:3].add(lame_first * (strain[0] + strain[1] + strain[2]))
    return return_map(stress + time_step * increment, branch_flags)


def pad_last(field):
    return jnp.pad(field, ((0, 0), (0, 0), (0, 0), (1, 1)))


def selectors(indices, row_count, col_count):
    col_table = (
        (indices % col_count)[None, :] == jnp.arange(col_count, dtype=jnp.int32)[:, None]
    ).astype(jnp.float32)
    row_table = (
        (indices // col_count)[None, :] == jnp.arange(row_count, dtype=jnp.int32)[:, None]
    ).astype(jnp.float32)
    return (col_table, row_table)


def pick_values(table, col_table, row_table):
    row_count = row_table.shape[0]
    columns = jnp.dot(
        table, col_table, precision=lax.Precision.HIGHEST, preferred_element_type=jnp.float32
    )
    columns = columns.reshape(3, row_count, columns.shape[1])
    return jnp.sum(columns * row_table[None], axis=1)


def spread_values(values, col_table, row_table):
    row_count = row_table.shape[0]
    spread = (values[:, None, :] * row_table[None]).reshape(3 * row_count, values.shape[1])
    return lax.dot_general(
        spread,
        col_table,
        (((1,), (1,)), ((), ())),
        precision=lax.Precision.HIGHEST,
        preferred_element_type=jnp.float32,
    )


def contact_terms(flat_velocity, window, cell_index, elem_index, weight, cell_cols, pile_cols):
    cell_rows = flat_velocity.shape[1] // cell_cols
    pile_rows = window.shape[1] // pile_cols
    velocity_table = flat_velocity.reshape(3 * cell_rows, cell_cols)
    pile_table = window.reshape(3 * pile_rows, pile_cols)
    total = cell_index.shape[0]
    block = math.gcd(total, 512)
    blocks = total // block
    cell_blocks = cell_index.reshape(blocks, block)
    elem_blocks = elem_index.reshape(blocks, block)
    weight_blocks = weight.reshape(blocks, block)

    def one_block(carry, items):
        cell_sum, pile_sum = carry
        cell_ids, elem_ids, live = items
        cell_cols_table, cell_rows_table = selectors(cell_ids, cell_rows, cell_cols)
        pile_cols_table, pile_rows_table = selectors(elem_ids, pile_rows, pile_cols)
        at_cells = pick_values(velocity_table, cell_cols_table, cell_rows_table)
        at_pile = pick_values(pile_table, pile_cols_table, pile_rows_table)
        pushes = penalty * (at_pile - at_cells) * live[None, :]
        cell_sum = cell_sum + spread_values(pushes, cell_cols_table, cell_rows_table)
        pile_sum = pile_sum + spread_values(pushes, pile_cols_table, pile_rows_table)
        return ((cell_sum, pile_sum), None)

    start = (
        jnp.zeros((3 * cell_rows, cell_cols), jnp.float32),
        jnp.zeros((3 * pile_rows, pile_cols), jnp.float32),
    )
    (cell_sum, pile_sum), unused = lax.scan(
        one_block, start, (cell_blocks, elem_blocks, weight_blocks)
    )
    return (cell_sum.reshape(3, -1), pile_sum.reshape(3, -1))


def shards(
    stress,
    velocity,
    density,
    branch_flags,
    pile_velocity,
    pile_mass,
    jack_force,
    pair_elem,
    pair_cell,
):
    pile_width = pile_velocity.shape[1]
    cell_cols = velocity.shape[3]
    pile_cols = math.gcd(pile_width, 128)
    weight = (pair_cell >= 0).astype(jnp.float32).reshape(-1)
    cell_index = jnp.maximum(pair_cell, 0).reshape(-1)
    elem_index = pair_elem.reshape(-1)
    for step_number in range(STEPS):
        stress_padded = pad_last(extended(stress, (("depth", 1), ("plan", 2)), 1))
        stress_force = divergence(stress_padded)
        window = extended_2(pile_velocity, (("depth", 1),), pile_width)
        flat_velocity = velocity.reshape(3, -1)
        cell_terms, pile_terms = contact_terms(
            flat_velocity, window, cell_index, elem_index, weight, cell_cols, pile_cols
        )
        on_cells = cell_terms.reshape(velocity.shape)
        partial_value = pile_terms.reshape(3, 3, pile_width)
        summed = sent_and_summed(partial_value, "plan", 2)
        outgoing = jnp.stack([summed[:, 0], summed[:, 2]], axis=1)
        returned = extended_2(outgoing, (("depth", 1),), 1)
        on_pile = summed[:, 1] + returned[:, 0] + returned[:, 3]
        velocity = velocity + time_step * (stress_force + on_cells) / density
        share_width = on_pile.shape[1]
        first_index = lax.axis_index("plan") * share_width
        own_velocity = lax.dynamic_slice_in_dim(pile_velocity, first_index, share_width, 1)
        own_force = lax.dynamic_slice_in_dim(jack_force, first_index, share_width, 1)
        own_mass = lax.dynamic_slice_in_dim(pile_mass, first_index, share_width, 0)
        updated = own_velocity + time_step * (own_force - on_pile) / own_mass
        pile_velocity = gather_directly(updated, "plan", 1)
        velocity_padded = pad_last(extended(velocity, (("depth", 1), ("plan", 2)), 1))
        stress = stress_update(stress, velocity_padded, branch_flags)
    return (stress, velocity, pile_velocity)


def solution(mesh):
    placed = (
        P(None, "depth", "plan", None),
        P(None, "depth", "plan", None),
        P("depth", "plan", None),
        P("depth", "plan", None),
        P(None, "depth"),
        P("depth"),
        P(None, "depth"),
        P("depth", "plan"),
        P("depth", "plan"),
    )
    return jax.shard_map(
        shards,
        mesh=mesh,
        in_specs=placed,
        out_specs=(
            P(None, "depth", "plan", None),
            P(None, "depth", "plan", None),
            P(None, "depth"),
        ),
        check_vma=False,
    )
```

profile of v0, /device:TPU:256, one launch (start us, length us, event | category | flops | bytes accessed | tf_op | source)
XLA Modules:
  0.0 309.7 jit_solution(13990140386146032096)
XLA Ops:
  0.6 2.4 collective-permute-start.5
  3.1 2.0 collective-permute-start.4
  9.2 3.0 collective-permute-start.1
  12.3 4.3 %collective-permute-start.3 = (f32[6,8,1,256]{3,2,1,0:T(1,128)S(1)}, f32[6,8,1,256]{3,2,1,0:T(1,128)S(1)}, u32[]{:S(2)}, u32[]{:S(2)}) collective-permute-start(f32[6,8,1,256]{3,2,1,0:T(1,128)S(1)} %get-tuple-element.662), channel_id=1, source_target_pairs={{0,1},{1,2},{2,3},{3,4},{4,5},{5,6},{6,7},{7,8},{8,9},{9,10},{10,1... | collective-permute-start | bytes 147464 | tf_op jit(solution)/shard_map/ppermute | solution.py:27
  19.8 7.0 %collective-permute-start = (f32[6,1,16,256]{3,2,1,0:T(8,128)}, f32[6,1,16,256]{3,2,1,0:T(8,128)S(1)}, u32[]{:S(2)}, u32[]{:S(2)}) collective-permute-start(f32[6,1,16,256]{3,2,1,0:T(8,128)} %get-tuple-element.664), channel_id=1, source_target_pairs={{16,0},{32,16},{48,32},{64,48},{80,64},{96,80},{112,96},{128,112},... | collective-permute-start | bytes 294920 | tf_op jit(solution)/shard_map/ppermute | solution.py:28
  28.1 12.2 %while.51 = (s32[]{:T(128)}, f32[384,256]{1,0:T(8,128)S(1)}, f32[432,128]{1,0:T(8,128)S(1)}, s32[4,512]{1,0:T(4,128)S(1)}, f32[432,128]{1,0:T(8,128)S(1)}, /*ind...) while((s32[]{:T(128)}, f32[384,256]{1,0:T(8,128)S(1)}, ...), condition=%wide.region_3.4_spmd.clone, body=%wide.region_0.3_spmd.clone.sunk | while | flops 1889689600 | bytes 10281088 | solution.py:211
  44.7 5.4 %collective-permute-start.9 = (f32[3,8,1,256]{3,2,1,0:T(1,128)S(1)}, f32[3,8,1,256]{3,2,1,0:T(1,128)S(1)}, u32[]{:S(2)}, u32[]{:S(2)}) collective-permute-start(f32[3,8,1,256]{3,2,1,0:T(1,128)S(1)} %get-tuple-element.681), channel_id=1, source_target_pairs={{0,1},{1,2},{2,3},{3,4},{4,5},{5,6},{6,7},{7,8},{8,9},{9,10},{10,1... | collective-permute-start | bytes 73736 | tf_op jit(solution)/shard_map/ppermute | solution.py:27
  50.2 2.1 collective-permute-start.6
  52.3 2.2 collective-permute-start.7
  55.5 9.8 %all-to-all-start = ((f32[16,3,3,384]{3,2,1,0:T(4,128)}), f32[16,3,3,384]{3,2,1,0:T(4,128)S(1)}, u32[]{:S(2)}, u32[]{:S(2)}) async-start(f32[16,3,3,384]{3,2,1,0:T(4,128)} %copy.21), calls=%async_computation | async-start | bytes 589824 | tf_op jit(solution)/shard_map/all_to_all | solution.py:59
  69.2 7.1 %collective-permute-start.10 = (f32[6,1,16,256]{3,2,1,0:T(8,128)S(1)}, f32[6,1,16,256]{3,2,1,0:T(8,128)S(1)}, u32[]{:S(2)}, u32[]{:S(2)}) collective-permute-start(f32[6,1,16,256]{3,2,1,0:T(8,128)S(1)} %get-tuple-element.655), channel_id=1, source_target_pairs={{16,0},{32,16},{48,32},{64,48},{80,64},{96,80},{112,96},{128,112},... | collective-permute-start | bytes 294920 | tf_op jit(solution)/shard_map/ppermute | solution.py:28
  76.3 1.9 collective-permute-start.11
  79.6 4.5 %collective-permute-start.13 = (f32[6,8,1,256]{3,2,1,0:T(1,128)S(1)}, f32[6,8,1,256]{3,2,1,0:T(1,128)S(1)}, u32[]{:S(2)}, u32[]{:S(2)}) collective-permute-start(f32[6,8,1,256]{3,2,1,0:T(1,128)S(1)} %get-tuple-element.656), channel_id=1, source_target_pairs={{0,1},{1,2},{2,3},{3,4},{4,5},{5,6},{6,7},{7,8},{8,9},{9,10},{10,1... | collective-permute-start | bytes 147464 | tf_op jit(solution)/shard_map/ppermute | solution.py:27
  86.9 2.5 select_maximum_fusion.4
  89.5 5.8 %collective-permute-start.15 = (f32[3,1,384]{2,1,0:T(1,128)S(1)}, f32[3,1,384]{2,1,0:T(1,128)S(1)}, u32[]{:S(2)}, u32[]{:S(2)}) collective-permute-start(f32[3,1,384]{2,1,0:T(1,128)S(1)} %get-tuple-element.693), channel_id=1, source_target_pairs={{16,0},{32,16},{48,32},{64,48},{80,64},{96,80},{112,96},{128,112},... | collective-permute-start | bytes 13832 | tf_op jit(solution)/shard_map/ppermute | solution.py:47
  95.3 1.9 collective-permute-start.14
  97.2 2.2 fusion.34
  99.4 5.0 %collective-permute-done.14 = f32[3,1,384]{2,1,0:T(1,128)S(1)} collective-permute-done((f32[3,1,384]{2,1,0:T(1,128)S(1)}, f32[3,1,384]{2,1,0:T(1,128)S(1)}, u32[]{:S(2)}, u32[]{:S(2)}) %collective-permute-start.14) | collective-permute-done | bytes 4640 | tf_op jit(solution)/shard_map/ppermute | solution.py:44
  105.8 10.5 %all-to-all-start.1 = ((f32[16,3,384]{2,1,0:T(4,128)}), f32[16,3,384]{2,1,0:T(4,128)S(1)}, u32[]{:S(2)}, u32[]{:S(2)}) async-start(f32[16,3,384]{2,1,0:T(4,128)} %broadcast_in_dim.33), calls=%async_computation.1 | async-start | bytes 196608 | tf_op jit(solution)/shard_map/all_to_all | solution.py:65
  117.8 7.9 %all-to-all-done.1 = f32[16,3,384]{2,1,0:T(4,128)S(1)} async-done(((f32[16,3,384]{2,1,0:T(4,128)}), f32[16,3,384]{2,1,0:T(4,128)S(1)}, u32[]{:S(2)}, u32[]{:S(2)}) %all-to-all-start.1) | async-done | bytes 73760 | tf_op jit(solution)/shard_map/all_to_all | solution.py:65
  127.6 2.6 collective-permute-start.16
  130.2 2.0 slice_add_fusion.19
  132.2 5.7 %collective-permute-done.16 = f32[3,6144]{1,0:T(4,128)S(1)} collective-permute-done((f32[3,6144]{1,0:T(4,128)S(1)}, f32[3,6144]{1,0:T(4,128)S(1)}, u32[]{:S(2)}, u32[]{:S(2)}) %collective-permute-start.16) | collective-permute-done | bytes 73760 | tf_op jit(solution)/shard_map/ppermute | solution.py:44
  138.1 12.3 %while.52 = (s32[]{:T(128)}, f32[384,256]{1,0:T(8,128)S(1)}, f32[432,128]{1,0:T(8,128)S(1)}, s32[4,512]{1,0:T(4,128)S(1)}, f32[432,128]{1,0:T(8,128)S(1)}, /*ind...) while((s32[]{:T(128)}, f32[384,256]{1,0:T(8,128)S(1)}, ...), condition=%wide.region_8.9_spmd.clone, body=%wide.region_5.8_spmd.clone.sunk | while | flops 1889689600 | bytes 10281088 | solution.py:211
  151.5 1.9 collective-permute-start.18
  153.5 2.4 collective-permute-start.19
  155.9 3.5 %collective-permute-start.21 = (f32[3,8,1,256]{3,2,1,0:T(1,128)S(1)}, f32[3,8,1,256]{3,2,1,0:T(1,128)S(1)}, u32[]{:S(2)}, u32[]{:S(2)}) collective-permute-start(f32[3,8,1,256]{3,2,1,0:T(1,128)S(1)} %get-tuple-element.677), channel_id=1, source_target_pairs={{0,1},{1,2},{2,3},{3,4},{4,5},{5,6},{6,7},{7,8},{8,9},{9,10},{10,1... | collective-permute-start | bytes 73736 | tf_op jit(solution)/shard_map/ppermute | solution.py:27
  161.7 5.3 %all-to-all-start.2 = ((f32[16,3,3,384]{3,2,1,0:T(4,128)}), f32[16,3,3,384]{3,2,1,0:T(4,128)S(1)}, u32[]{:S(2)}, u32[]{:S(2)}) async-start(f32[16,3,3,384]{3,2,1,0:T(4,128)} %copy.23), calls=%async_computation.2 | async-start | bytes 589824 | tf_op jit(solution)/shard_map/all_to_all | solution.py:59
  170.9 6.5 %collective-permute-start.22 = (f32[6,1,16,256]{3,2,1,0:T(8,128)S(1)}, f32[6,1,16,256]{3,2,1,0:T(8,128)S(1)}, u32[]{:S(2)}, u32[]{:S(2)}) collective-permute-start(f32[6,1,16,256]{3,2,1,0:T(8,128)S(1)} %get-tuple-element.649), channel_id=1, source_target_pairs={{16,0},{32,16},{48,32},{64,48},{80,64},{96,80},{112,96},{128,112},... | collective-permute-start | bytes 294920 | tf_op jit(solution)/shard_map/ppermute | solution.py:28
  180.7 4.5 %collective-permute-start.25 = (f32[6,8,1,256]{3,2,1,0:T(1,128)S(1)}, f32[6,8,1,256]{3,2,1,0:T(1,128)S(1)}, u32[]{:S(2)}, u32[]{:S(2)}) collective-permute-start(f32[6,8,1,256]{3,2,1,0:T(1,128)S(1)} %get-tuple-element.650), channel_id=1, source_target_pairs={{0,1},{1,2},{2,3},{3,4},{4,5},{5,6},{6,7},{7,8},{8,9},{9,10},{10,1... | collective-permute-start | bytes 147464 | tf_op jit(solution)/shard_map/ppermute | solution.py:27
  188.0 2.5 select_maximum_fusion
  190.6 5.8 %collective-permute-start.27 = (f32[3,1,384]{2,0,1:T(4,128)S(1)}, f32[3,1,384]{2,0,1:T(4,128)S(1)}, u32[]{:S(2)}, u32[]{:S(2)}) collective-permute-start(f32[3,1,384]{2,0,1:T(4,128)S(1)} %copy.42), channel_id=1, source_target_pairs={{16,0},{32,16},{48,32},{64,48},{80,64},{96,80},{112,96},{128,112},... | collective-permute-start | bytes 13832 | tf_op jit(solution)/shard_map/ppermute | solution.py:47
  198.4 2.2 fusion.29
  200.5 5.1 %collective-permute-done.26 = f32[3,1,384]{2,0,1:T(4,128)S(1)} collective-permute-done((f32[3,1,384]{2,0,1:T(4,128)S(1)}, f32[3,1,384]{2,0,1:T(4,128)S(1)}, u32[]{:S(2)}, u32[]{:S(2)}) %collective-permute-start.26) | collective-permute-done | bytes 4640 | tf_op jit(solution)/shard_map/ppermute | solution.py:44
  207.0 10.5 %all-to-all-start.3 = ((f32[16,3,384]{2,1,0:T(4,128)}), f32[16,3,384]{2,1,0:T(4,128)S(1)}, u32[]{:S(2)}, u32[]{:S(2)}) async-start(f32[16,3,384]{2,1,0:T(4,128)} %broadcast_in_dim.34), calls=%async_computation.3 | async-start | bytes 196608 | tf_op jit(solution)/shard_map/all_to_all | solution.py:65
  219.0 7.9 %all-to-all-done.3 = f32[16,3,384]{2,1,0:T(4,128)S(1)} async-done(((f32[16,3,384]{2,1,0:T(4,128)}), f32[16,3,384]{2,1,0:T(4,128)S(1)}, u32[]{:S(2)}, u32[]{:S(2)}) %all-to-all-start.3) | async-done | bytes 73760 | tf_op jit(solution)/shard_map/all_to_all | solution.py:65
  228.8 2.6 collective-permute-start.28
  231.4 2.0 slice_add_fusion.10
  233.4 5.6 %collective-permute-done.28 = f32[3,6144]{1,0:T(4,128)S(1)} collective-permute-done((f32[3,6144]{1,0:T(4,128)S(1)}, f32[3,6144]{1,0:T(4,128)S(1)}, u32[]{:S(2)}, u32[]{:S(2)}) %collective-permute-start.28) | collective-permute-done | bytes 73760 | tf_op jit(solution)/shard_map/ppermute | solution.py:44
  239.3 12.3 %while.53 = (s32[]{:T(128)}, f32[384,256]{1,0:T(8,128)S(1)}, f32[432,128]{1,0:T(8,128)S(1)}, s32[4,512]{1,0:T(4,128)S(1)}, f32[432,128]{1,0:T(8,128)S(1)}, /*ind...) while((s32[]{:T(128)}, f32[384,256]{1,0:T(8,128)S(1)}, ...), condition=%wide.region_13.14_spmd.clone, body=%wide.region_10.13_spmd.clone.sunk | while | flops 1889689600 | bytes 10281088 | solution.py:211
  254.6 2.4 collective-permute-start.31
  258.4 4.5 %collective-permute-start.33 = (f32[3,8,1,256]{3,2,1,0:T(1,128)S(1)}, f32[3,8,1,256]{3,2,1,0:T(1,128)S(1)}, u32[]{:S(2)}, u32[]{:S(2)}) collective-permute-start(f32[3,8,1,256]{3,2,1,0:T(1,128)S(1)} %get-tuple-element.673), channel_id=1, source_target_pairs={{0,1},{1,2},{2,3},{3,4},{4,5},{5,6},{6,7},{7,8},{8,9},{9,10},{10,1... | collective-permute-start | bytes 73736 | tf_op jit(solution)/shard_map/ppermute | solution.py:27
  263.8 5.2 %all-to-all-start.4 = ((f32[16,3,3,384]{3,2,1,0:T(4,128)}), f32[16,3,3,384]{3,2,1,0:T(4,128)S(1)}, u32[]{:S(2)}, u32[]{:S(2)}) async-start(f32[16,3,3,384]{3,2,1,0:T(4,128)} %copy.28), calls=%async_computation.4 | async-start | bytes 589824 | tf_op jit(solution)/shard_map/all_to_all | solution.py:59
  270.8 10.6 %all-to-all-done.4 = f32[16,3,3,384]{3,2,1,0:T(4,128)S(1)} async-done(((f32[16,3,3,384]{3,2,1,0:T(4,128)}), f32[16,3,3,384]{3,2,1,0:T(4,128)S(1)}, u32[]{:S(2)}, u32[]{:S(2)}) %all-to-all-start.4) | async-done | bytes 221216 | tf_op jit(solution)/shard_map/all_to_all | solution.py:59
  281.5 4.0 %collective-permute-start.35 = (f32[3,1,384]{2,0,1:T(4,128)S(1)}, f32[3,1,384]{2,0,1:T(4,128)S(1)}, u32[]{:S(2)}, u32[]{:S(2)}) collective-permute-start(f32[3,1,384]{2,0,1:T(4,128)S(1)} %copy.45), channel_id=1, source_target_pairs={{16,0},{32,16},{48,32},{64,48},{80,64},{96,80},{112,96},{128,112},... | collective-permute-start | bytes 13832 | tf_op jit(solution)/shard_map/ppermute | solution.py:47
  287.6 7.2 %collective-permute-done.34 = f32[3,1,384]{2,0,1:T(4,128)S(1)} collective-permute-done((f32[3,1,384]{2,0,1:T(4,128)S(1)}, f32[3,1,384]{2,0,1:T(4,128)S(1)}, u32[]{:S(2)}, u32[]{:S(2)}) %collective-permute-start.34) | collective-permute-done | bytes 4640 | tf_op jit(solution)/shard_map/ppermute | solution.py:44
  296.1 3.5 %all-to-all-start.5 = ((f32[16,3,384]{2,1,0:T(4,128)}), f32[16,3,384]{2,1,0:T(4,128)S(1)}, u32[]{:S(2)}, u32[]{:S(2)}) async-start(f32[16,3,384]{2,1,0:T(4,128)} %broadcast_in_dim.35), calls=%async_computation.5 | async-start | bytes 196608 | tf_op jit(solution)/shard_map/all_to_all | solution.py:65
  300.8 8.2 %all-to-all-done.5 = f32[16,3,384]{2,1,0:T(4,128)S(1)} async-done(((f32[16,3,384]{2,1,0:T(4,128)}), f32[16,3,384]{2,1,0:T(4,128)S(1)}, u32[]{:S(2)}, u32[]{:S(2)}) %all-to-all-start.5) | async-done | bytes 73760 | tf_op jit(solution)/shard_map/all_to_all | solution.py:65
  (389 shorter events, 94.2 us)
Async XLA Ops:
  0.6 27.5 %copy-start = (f32[3,8,16,256]{3,2,1,0:T(8,128)S(1)}, f32[3,8,16,256]{3,2,1,0:T(8,128)}, u32[]{:S(2)}) copy-start(f32[3,8,16,256]{3,2,1,0:T(8,128)} %param.22) | copy-start | bytes 1179652
  0.6 26.3 %collective-permute-start.5 = (f32[3,6144]{1,0:T(4,128)}, f32[3,6144]{1,0:T(4,128)S(1)}, u32[]{:S(2)}, u32[]{:S(2)}) collective-permute-start(f32[3,6144]{1,0:T(4,128)} %param.25), channel_id=1, source_target_pairs={{16,0},{32,16},{48,32},{64,48},{80,64},{96,80},{112,96},{128,112},... | collective-permute-start | bytes 221192 | tf_op jit(solution)/shard_map/ppermute | solution.py:47
  3.1 23.9 %collective-permute-start.4 = (f32[3,6144]{1,0:T(4,128)}, f32[3,6144]{1,0:T(4,128)S(1)}, u32[]{:S(2)}, u32[]{:S(2)}) collective-permute-start(f32[3,6144]{1,0:T(4,128)} %param.25), channel_id=1, source_target_pairs={{0,16},{16,32},{32,48},{48,64},{64,80},{80,96},{96,112},{112,128},... | collective-permute-start | bytes 221192 | tf_op jit(solution)/shard_map/ppermute | solution.py:44
  6.3 13.5 %collective-permute-start.2 = (f32[6,8,1,256]{3,2,1,0:T(1,128)S(1)}, f32[6,8,1,256]{3,2,1,0:T(1,128)S(1)}, u32[]{:S(2)}, u32[]{:S(2)}) collective-permute-start(f32[6,8,1,256]{3,2,1,0:T(1,128)S(1)} %get-tuple-element.663), channel_id=1, source_target_pairs={{1,0},{2,1},{3,2},{4,3},{5,4},{6,5},{7,6},{8,7},{9,8},{10,9},{11,1... | collective-permute-start | bytes 147464 | tf_op jit(solution)/shard_map/ppermute | solution.py:28
  9.2 31.1 %collective-permute-start.1 = (f32[6,1,16,256]{3,2,1,0:T(8,128)}, f32[6,1,16,256]{3,2,1,0:T(8,128)S(1)}, u32[]{:S(2)}, u32[]{:S(2)}) collective-permute-start(f32[6,1,16,256]{3,2,1,0:T(8,128)} %get-tuple-element.665), channel_id=1, source_target_pairs={{0,16},{16,32},{32,48},{48,64},{64,80},{80,96},{96,112},{112,128},... | collective-permute-start | bytes 294920 | tf_op jit(solution)/shard_map/ppermute | solution.py:27
  12.3 14.7 %collective-permute-start.3 = (f32[6,8,1,256]{3,2,1,0:T(1,128)S(1)}, f32[6,8,1,256]{3,2,1,0:T(1,128)S(1)}, u32[]{:S(2)}, u32[]{:S(2)}) collective-permute-start(f32[6,8,1,256]{3,2,1,0:T(1,128)S(1)} %get-tuple-element.662), channel_id=1, source_target_pairs={{0,1},{1,2},{2,3},{3,4},{4,5},{5,6},{6,7},{7,8},{8,9},{9,10},{10,1... | collective-permute-start | bytes 147464 | tf_op jit(solution)/shard_map/ppermute | solution.py:27
  19.8 20.6 %collective-permute-start = (f32[6,1,16,256]{3,2,1,0:T(8,128)}, f32[6,1,16,256]{3,2,1,0:T(8,128)S(1)}, u32[]{:S(2)}, u32[]{:S(2)}) collective-permute-start(f32[6,1,16,256]{3,2,1,0:T(8,128)} %get-tuple-element.664), channel_id=1, source_target_pairs={{16,0},{32,16},{48,32},{64,48},{80,64},{96,80},{112,96},{128,112},... | collective-permute-start | bytes 294920 | tf_op jit(solution)/shard_map/ppermute | solution.py:28
  28.1 12.3 %copy-start.6 = (f32[6,8,16,256]{3,2,1,0:T(8,128)S(1)}, f32[6,8,16,256]{3,2,1,0:T(8,128)}, u32[]{:S(2)}) copy-start(f32[6,8,16,256]{3,2,1,0:T(8,128)} %param.21) | copy-start | bytes 2359300
  42.4 12.1 %copy-start.10 = (s32[8,16,256]{2,1,0:T(8,128)S(1)}, s32[8,16,256]{2,1,0:T(8,128)}, u32[]{:S(2)}) copy-start(s32[8,16,256]{2,1,0:T(8,128)} %param.24) | copy-start | bytes 393220
  43.4 21.8 %collective-permute-start.8 = (f32[3,8,1,256]{3,2,1,0:T(1,128)S(1)}, f32[3,8,1,256]{3,2,1,0:T(1,128)S(1)}, u32[]{:S(2)}, u32[]{:S(2)}) collective-permute-start(f32[3,8,1,256]{3,2,1,0:T(1,128)S(1)} %get-tuple-element.680), channel_id=1, source_target_pairs={{1,0},{2,1},{3,2},{4,3},{5,4},{6,5},{7,6},{8,7},{9,8},{10,9},{11,1... | collective-permute-start | bytes 73736 | tf_op jit(solution)/shard_map/ppermute | solution.py:28
  44.7 20.5 %collective-permute-start.9 = (f32[3,8,1,256]{3,2,1,0:T(1,128)S(1)}, f32[3,8,1,256]{3,2,1,0:T(1,128)S(1)}, u32[]{:S(2)}, u32[]{:S(2)}) collective-permute-start(f32[3,8,1,256]{3,2,1,0:T(1,128)S(1)} %get-tuple-element.681), channel_id=1, source_target_pairs={{0,1},{1,2},{2,3},{3,4},{4,5},{5,6},{6,7},{7,8},{8,9},{9,10},{10,1... | collective-permute-start | bytes 73736 | tf_op jit(solution)/shard_map/ppermute | solution.py:27
  50.2 15.1 %collective-permute-start.6 = (f32[3,1,16,256]{3,2,1,0:T(8,128)S(1)}, f32[3,1,16,256]{3,2,1,0:T(8,128)S(1)}, u32[]{:S(2)}, u32[]{:S(2)}) collective-permute-start(f32[3,1,16,256]{3,2,1,0:T(8,128)S(1)} %get-tuple-element.682), channel_id=1, source_target_pairs={{16,0},{32,16},{48,32},{64,48},{80,64},{96,80},{112,96},{128,112},... | collective-permute-start | bytes 147464 | tf_op jit(solution)/shard_map/ppermute | solution.py:28
  52.3 13.0 %collective-permute-start.7 = (f32[3,1,16,256]{3,2,1,0:T(8,128)S(1)}, f32[3,1,16,256]{3,2,1,0:T(8,128)S(1)}, u32[]{:S(2)}, u32[]{:S(2)}) collective-permute-start(f32[3,1,16,256]{3,2,1,0:T(8,128)S(1)} %get-tuple-element.683), channel_id=1, source_target_pairs={{0,16},{16,32},{32,48},{48,64},{64,80},{80,96},{96,112},{112,128},... | collective-permute-start | bytes 147464 | tf_op jit(solution)/shard_map/ppermute | solution.py:27
  55.5 33.9 %all-to-all-start = ((f32[16,3,3,384]{3,2,1,0:T(4,128)}), f32[16,3,3,384]{3,2,1,0:T(4,128)S(1)}, u32[]{:S(2)}, u32[]{:S(2)}) async-start(f32[16,3,3,384]{3,2,1,0:T(4,128)} %copy.21), calls=%async_computation | async-start | bytes 589824 | tf_op jit(solution)/shard_map/all_to_all | solution.py:59
  69.2 16.7 %collective-permute-start.10 = (f32[6,1,16,256]{3,2,1,0:T(8,128)S(1)}, f32[6,1,16,256]{3,2,1,0:T(8,128)S(1)}, u32[]{:S(2)}, u32[]{:S(2)}) collective-permute-start(f32[6,1,16,256]{3,2,1,0:T(8,128)S(1)} %get-tuple-element.655), channel_id=1, source_target_pairs={{16,0},{32,16},{48,32},{64,48},{80,64},{96,80},{112,96},{128,112},... | collective-permute-start | bytes 294920 | tf_op jit(solution)/shard_map/ppermute | solution.py:28
  76.3 10.6 %collective-permute-start.11 = (f32[6,1,16,256]{3,2,1,0:T(8,128)S(1)}, f32[6,1,16,256]{3,2,1,0:T(8,128)S(1)}, u32[]{:S(2)}, u32[]{:S(2)}) collective-permute-start(f32[6,1,16,256]{3,2,1,0:T(8,128)S(1)} %get-tuple-element.654), channel_id=1, source_target_pairs={{0,16},{16,32},{32,48},{48,64},{64,80},{80,96},{96,112},{112,128},... | collective-permute-start | bytes 294920 | tf_op jit(solution)/shard_map/ppermute | solution.py:27
  78.3 6.7 %collective-permute-start.12 = (f32[6,8,1,256]{3,2,1,0:T(1,128)S(1)}, f32[6,8,1,256]{3,2,1,0:T(1,128)S(1)}, u32[]{:S(2)}, u32[]{:S(2)}) collective-permute-start(f32[6,8,1,256]{3,2,1,0:T(1,128)S(1)} %get-tuple-element.657), channel_id=1, source_target_pairs={{1,0},{2,1},{3,2},{4,3},{5,4},{6,5},{7,6},{8,7},{9,8},{10,9},{11,1... | collective-permute-start | bytes 147464 | tf_op jit(solution)/shard_map/ppermute | solution.py:28
  79.6 6.3 %collective-permute-start.13 = (f32[6,8,1,256]{3,2,1,0:T(1,128)S(1)}, f32[6,8,1,256]{3,2,1,0:T(1,128)S(1)}, u32[]{:S(2)}, u32[]{:S(2)}) collective-permute-start(f32[6,8,1,256]{3,2,1,0:T(1,128)S(1)} %get-tuple-element.656), channel_id=1, source_target_pairs={{0,1},{1,2},{2,3},{3,4},{4,5},{5,6},{6,7},{7,8},{8,9},{9,10},{10,1... | collective-permute-start | bytes 147464 | tf_op jit(solution)/shard_map/ppermute | solution.py:27
  89.5 9.9 %collective-permute-start.15 = (f32[3,1,384]{2,1,0:T(1,128)S(1)}, f32[3,1,384]{2,1,0:T(1,128)S(1)}, u32[]{:S(2)}, u32[]{:S(2)}) collective-permute-start(f32[3,1,384]{2,1,0:T(1,128)S(1)} %get-tuple-element.693), channel_id=1, source_target_pairs={{16,0},{32,16},{48,32},{64,48},{80,64},{96,80},{112,96},{128,112},... | collective-permute-start | bytes 13832 | tf_op jit(solution)/shard_map/ppermute | solution.py:47
  95.3 9.2 %collective-permute-start.14 = (f32[3,1,384]{2,1,0:T(1,128)S(1)}, f32[3,1,384]{2,1,0:T(1,128)S(1)}, u32[]{:S(2)}, u32[]{:S(2)}) collective-permute-start(f32[3,1,384]{2,1,0:T(1,128)S(1)} %get-tuple-element.692), channel_id=1, source_target_pairs={{0,16},{16,32},{32,48},{48,64},{64,80},{80,96},{96,112},{112,128},... | collective-permute-start | bytes 13832 | tf_op jit(solution)/shard_map/ppermute | solution.py:44
  105.8 19.9 %all-to-all-start.1 = ((f32[16,3,384]{2,1,0:T(4,128)}), f32[16,3,384]{2,1,0:T(4,128)S(1)}, u32[]{:S(2)}, u32[]{:S(2)}) async-start(f32[16,3,384]{2,1,0:T(4,128)} %broadcast_in_dim.33), calls=%async_computation.1 | async-start | bytes 196608 | tf_op jit(solution)/shard_map/all_to_all | solution.py:65
  125.7 12.4 %copy-start.8 = (f32[16,3,384]{2,1,0:T(4,128)}, f32[16,3,384]{2,1,0:T(4,128)S(1)}, u32[]{:S(2)}) copy-start(f32[16,3,384]{2,1,0:T(4,128)S(1)} %all-to-all-done.1) | copy-start | bytes 221188
  125.7 6.5 %collective-permute-start.17 = (f32[3,6144]{1,0:T(4,128)S(1)}, f32[3,6144]{1,0:T(4,128)S(1)}, u32[]{:S(2)}, u32[]{:S(2)}) collective-permute-start(f32[3,6144]{1,0:T(4,128)S(1)} %bitcast.217), channel_id=1, source_target_pairs={{16,0},{32,16},{48,32},{64,48},{80,64},{96,80},{112,96},{128,112},... | collective-permute-start | bytes 221192 | tf_op jit(solution)/shard_map/ppermute | solution.py:47
  127.6 10.3 %collective-permute-start.16 = (f32[3,6144]{1,0:T(4,128)S(1)}, f32[3,6144]{1,0:T(4,128)S(1)}, u32[]{:S(2)}, u32[]{:S(2)}) collective-permute-start(f32[3,6144]{1,0:T(4,128)S(1)} %bitcast.218), channel_id=1, source_target_pairs={{0,16},{16,32},{32,48},{48,64},{64,80},{80,96},{96,112},{112,128},... | collective-permute-start | bytes 221192 | tf_op jit(solution)/shard_map/ppermute | solution.py:44
  151.5 15.5 %collective-permute-start.18 = (f32[3,1,16,256]{3,2,1,0:T(8,128)S(1)}, f32[3,1,16,256]{3,2,1,0:T(8,128)S(1)}, u32[]{:S(2)}, u32[]{:S(2)}) collective-permute-start(f32[3,1,16,256]{3,2,1,0:T(8,128)S(1)} %get-tuple-element.678), channel_id=1, source_target_pairs={{16,0},{32,16},{48,32},{64,48},{80,64},{96,80},{112,96},{128,112},... | collective-permute-start | bytes 147464 | tf_op jit(solution)/shard_map/ppermute | solution.py:28
  153.5 13.6 %collective-permute-start.19 = (f32[3,1,16,256]{3,2,1,0:T(8,128)S(1)}, f32[3,1,16,256]{3,2,1,0:T(8,128)S(1)}, u32[]{:S(2)}, u32[]{:S(2)}) collective-permute-start(f32[3,1,16,256]{3,2,1,0:T(8,128)S(1)} %get-tuple-element.679), channel_id=1, source_target_pairs={{0,16},{16,32},{32,48},{48,64},{64,80},{80,96},{96,112},{112,128},... | collective-permute-start | bytes 147464 | tf_op jit(solution)/shard_map/ppermute | solution.py:27
  155.9 11.0 %collective-permute-start.21 = (f32[3,8,1,256]{3,2,1,0:T(1,128)S(1)}, f32[3,8,1,256]{3,2,1,0:T(1,128)S(1)}, u32[]{:S(2)}, u32[]{:S(2)}) collective-permute-start(f32[3,8,1,256]{3,2,1,0:T(1,128)S(1)} %get-tuple-element.677), channel_id=1, source_target_pairs={{0,1},{1,2},{2,3},{3,4},{4,5},{5,6},{6,7},{7,8},{8,9},{9,10},{10,1... | collective-permute-start | bytes 73736 | tf_op jit(solution)/shard_map/ppermute | solution.py:27
  159.5 7.5 %collective-permute-start.20 = (f32[3,8,1,256]{3,2,1,0:T(1,128)S(1)}, f32[3,8,1,256]{3,2,1,0:T(1,128)S(1)}, u32[]{:S(2)}, u32[]{:S(2)}) collective-permute-start(f32[3,8,1,256]{3,2,1,0:T(1,128)S(1)} %get-tuple-element.676), channel_id=1, source_target_pairs={{1,0},{2,1},{3,2},{4,3},{5,4},{6,5},{7,6},{8,7},{9,8},{10,9},{11,1... | collective-permute-start | bytes 73736 | tf_op jit(solution)/shard_map/ppermute | solution.py:28
  161.7 28.8 %all-to-all-start.2 = ((f32[16,3,3,384]{3,2,1,0:T(4,128)}), f32[16,3,3,384]{3,2,1,0:T(4,128)S(1)}, u32[]{:S(2)}, u32[]{:S(2)}) async-start(f32[16,3,3,384]{3,2,1,0:T(4,128)} %copy.23), calls=%async_computation.2 | async-start | bytes 589824 | tf_op jit(solution)/shard_map/all_to_all | solution.py:59
  170.9 16.2 %collective-permute-start.22 = (f32[6,1,16,256]{3,2,1,0:T(8,128)S(1)}, f32[6,1,16,256]{3,2,1,0:T(8,128)S(1)}, u32[]{:S(2)}, u32[]{:S(2)}) collective-permute-start(f32[6,1,16,256]{3,2,1,0:T(8,128)S(1)} %get-tuple-element.649), channel_id=1, source_target_pairs={{16,0},{32,16},{48,32},{64,48},{80,64},{96,80},{112,96},{128,112},... | collective-permute-start | bytes 294920 | tf_op jit(solution)/shard_map/ppermute | solution.py:28
  177.4 10.6 %collective-permute-start.23 = (f32[6,1,16,256]{3,2,1,0:T(8,128)S(1)}, f32[6,1,16,256]{3,2,1,0:T(8,128)S(1)}, u32[]{:S(2)}, u32[]{:S(2)}) collective-permute-start(f32[6,1,16,256]{3,2,1,0:T(8,128)S(1)} %get-tuple-element.648), channel_id=1, source_target_pairs={{0,16},{16,32},{32,48},{48,64},{64,80},{80,96},{96,112},{112,128},... | collective-permute-start | bytes 294920 | tf_op jit(solution)/shard_map/ppermute | solution.py:27
  179.4 6.0 %collective-permute-start.24 = (f32[6,8,1,256]{3,2,1,0:T(1,128)S(1)}, f32[6,8,1,256]{3,2,1,0:T(1,128)S(1)}, u32[]{:S(2)}, u32[]{:S(2)}) collective-permute-start(f32[6,8,1,256]{3,2,1,0:T(1,128)S(1)} %get-tuple-element.651), channel_id=1, source_target_pairs={{1,0},{2,1},{3,2},{4,3},{5,4},{6,5},{7,6},{8,7},{9,8},{10,9},{11,1... | collective-permute-start | bytes 147464 | tf_op jit(solution)/shard_map/ppermute | solution.py:28
  180.7 6.3 %collective-permute-start.25 = (f32[6,8,1,256]{3,2,1,0:T(1,128)S(1)}, f32[6,8,1,256]{3,2,1,0:T(1,128)S(1)}, u32[]{:S(2)}, u32[]{:S(2)}) collective-permute-start(f32[6,8,1,256]{3,2,1,0:T(1,128)S(1)} %get-tuple-element.650), channel_id=1, source_target_pairs={{0,1},{1,2},{2,3},{3,4},{4,5},{5,6},{6,7},{7,8},{8,9},{9,10},{10,1... | collective-permute-start | bytes 147464 | tf_op jit(solution)/shard_map/ppermute | solution.py:27
  190.6 9.9 %collective-permute-start.27 = (f32[3,1,384]{2,0,1:T(4,128)S(1)}, f32[3,1,384]{2,0,1:T(4,128)S(1)}, u32[]{:S(2)}, u32[]{:S(2)}) collective-permute-start(f32[3,1,384]{2,0,1:T(4,128)S(1)} %copy.42), channel_id=1, source_target_pairs={{16,0},{32,16},{48,32},{64,48},{80,64},{96,80},{112,96},{128,112},... | collective-permute-start | bytes 13832 | tf_op jit(solution)/shard_map/ppermute | solution.py:47
  196.4 9.2 %collective-permute-start.26 = (f32[3,1,384]{2,0,1:T(4,128)S(1)}, f32[3,1,384]{2,0,1:T(4,128)S(1)}, u32[]{:S(2)}, u32[]{:S(2)}) collective-permute-start(f32[3,1,384]{2,0,1:T(4,128)S(1)} %copy.41), channel_id=1, source_target_pairs={{0,16},{16,32},{32,48},{48,64},{64,80},{80,96},{96,112},{112,128},... | collective-permute-start | bytes 13832 | tf_op jit(solution)/shard_map/ppermute | solution.py:44
  207.0 19.9 %all-to-all-start.3 = ((f32[16,3,384]{2,1,0:T(4,128)}), f32[16,3,384]{2,1,0:T(4,128)S(1)}, u32[]{:S(2)}, u32[]{:S(2)}) async-start(f32[16,3,384]{2,1,0:T(4,128)} %broadcast_in_dim.34), calls=%async_computation.3 | async-start | bytes 196608 | tf_op jit(solution)/shard_map/all_to_all | solution.py:65
  226.8 12.4 %copy-start.9 = (f32[16,3,384]{2,1,0:T(4,128)}, f32[16,3,384]{2,1,0:T(4,128)S(1)}, u32[]{:S(2)}) copy-start(f32[16,3,384]{2,1,0:T(4,128)S(1)} %all-to-all-done.3) | copy-start | bytes 221188
  226.8 6.5 %collective-permute-start.29 = (f32[3,6144]{1,0:T(4,128)S(1)}, f32[3,6144]{1,0:T(4,128)S(1)}, u32[]{:S(2)}, u32[]{:S(2)}) collective-permute-start(f32[3,6144]{1,0:T(4,128)S(1)} %bitcast.221), channel_id=1, source_target_pairs={{16,0},{32,16},{48,32},{64,48},{80,64},{96,80},{112,96},{128,112},... | collective-permute-start | bytes 221192 | tf_op jit(solution)/shard_map/ppermute | solution.py:47
  228.8 10.3 %collective-permute-start.28 = (f32[3,6144]{1,0:T(4,128)S(1)}, f32[3,6144]{1,0:T(4,128)S(1)}, u32[]{:S(2)}, u32[]{:S(2)}) collective-permute-start(f32[3,6144]{1,0:T(4,128)S(1)} %bitcast.222), channel_id=1, source_target_pairs={{0,16},{16,32},{32,48},{48,64},{64,80},{80,96},{96,112},{112,128},... | collective-permute-start | bytes 221192 | tf_op jit(solution)/shard_map/ppermute | solution.py:44
  252.7 17.3 %copy-start.5 = (f32[3,8,16,256]{3,2,1,0:T(8,128)}, f32[3,8,16,256]{3,2,1,0:T(8,128)S(1)}, u32[]{:S(2)}) copy-start(f32[3,8,16,256]{3,2,1,0:T(8,128)S(1)} %fusion.70) | copy-start | bytes 1179652
  252.7 16.4 %collective-permute-start.30 = (f32[3,1,16,256]{3,2,1,0:T(8,128)S(1)}, f32[3,1,16,256]{3,2,1,0:T(8,128)S(1)}, u32[]{:S(2)}, u32[]{:S(2)}) collective-permute-start(f32[3,1,16,256]{3,2,1,0:T(8,128)S(1)} %get-tuple-element.674), channel_id=1, source_target_pairs={{16,0},{32,16},{48,32},{64,48},{80,64},{96,80},{112,96},{128,112},... | collective-permute-start | bytes 147464 | tf_op jit(solution)/shard_map/ppermute | solution.py:28
  254.6 14.5 %collective-permute-start.31 = (f32[3,1,16,256]{3,2,1,0:T(8,128)S(1)}, f32[3,1,16,256]{3,2,1,0:T(8,128)S(1)}, u32[]{:S(2)}, u32[]{:S(2)}) collective-permute-start(f32[3,1,16,256]{3,2,1,0:T(8,128)S(1)} %get-tuple-element.675), channel_id=1, source_target_pairs={{0,16},{16,32},{32,48},{48,64},{64,80},{80,96},{96,112},{112,128},... | collective-permute-start | bytes 147464 | tf_op jit(solution)/shard_map/ppermute | solution.py:27
  257.1 12.0 %collective-permute-start.32 = (f32[3,8,1,256]{3,2,1,0:T(1,128)S(1)}, f32[3,8,1,256]{3,2,1,0:T(1,128)S(1)}, u32[]{:S(2)}, u32[]{:S(2)}) collective-permute-start(f32[3,8,1,256]{3,2,1,0:T(1,128)S(1)} %get-tuple-element.672), channel_id=1, source_target_pairs={{1,0},{2,1},{3,2},{4,3},{5,4},{6,5},{7,6},{8,7},{9,8},{10,9},{11,1... | collective-permute-start | bytes 73736 | tf_op jit(solution)/shard_map/ppermute | solution.py:28
  258.4 10.7 %collective-permute-start.33 = (f32[3,8,1,256]{3,2,1,0:T(1,128)S(1)}, f32[3,8,1,256]{3,2,1,0:T(1,128)S(1)}, u32[]{:S(2)}, u32[]{:S(2)}) collective-permute-start(f32[3,8,1,256]{3,2,1,0:T(1,128)S(1)} %get-tuple-element.673), channel_id=1, source_target_pairs={{0,1},{1,2},{2,3},{3,4},{4,5},{5,6},{6,7},{7,8},{8,9},{9,10},{10,1... | collective-permute-start | bytes 73736 | tf_op jit(solution)/shard_map/ppermute | solution.py:27
  263.8 17.6 %all-to-all-start.4 = ((f32[16,3,3,384]{3,2,1,0:T(4,128)}), f32[16,3,3,384]{3,2,1,0:T(4,128)S(1)}, u32[]{:S(2)}, u32[]{:S(2)}) async-start(f32[16,3,3,384]{3,2,1,0:T(4,128)} %copy.28), calls=%async_computation.4 | async-start | bytes 589824 | tf_op jit(solution)/shard_map/all_to_all | solution.py:59
  281.5 6.0 %collective-permute-start.35 = (f32[3,1,384]{2,0,1:T(4,128)S(1)}, f32[3,1,384]{2,0,1:T(4,128)S(1)}, u32[]{:S(2)}, u32[]{:S(2)}) collective-permute-start(f32[3,1,384]{2,0,1:T(4,128)S(1)} %copy.45), channel_id=1, source_target_pairs={{16,0},{32,16},{48,32},{64,48},{80,64},{96,80},{112,96},{128,112},... | collective-permute-start | bytes 13832 | tf_op jit(solution)/shard_map/ppermute | solution.py:47
  285.6 9.2 %collective-permute-start.34 = (f32[3,1,384]{2,0,1:T(4,128)S(1)}, f32[3,1,384]{2,0,1:T(4,128)S(1)}, u32[]{:S(2)}, u32[]{:S(2)}) collective-permute-start(f32[3,1,384]{2,0,1:T(4,128)S(1)} %copy.44), channel_id=1, source_target_pairs={{0,16},{16,32},{32,48},{48,64},{64,80},{80,96},{96,112},{112,128},... | collective-permute-start | bytes 13832 | tf_op jit(solution)/shard_map/ppermute | solution.py:44
  296.1 12.9 %all-to-all-start.5 = ((f32[16,3,384]{2,1,0:T(4,128)}), f32[16,3,384]{2,1,0:T(4,128)S(1)}, u32[]{:S(2)}, u32[]{:S(2)}) async-start(f32[16,3,384]{2,1,0:T(4,128)} %broadcast_in_dim.35), calls=%async_computation.5 | async-start | bytes 196608 | tf_op jit(solution)/shard_map/all_to_all | solution.py:65
  (7 other events, 7.4 us)
where the time goes:
time: 312 us; the launch traced here: 310 us
  starting transfers between devices  155 us (50%)
  waiting for transfers between devices  67.7 us (22%)
  other arithmetic  39.3 us (13%)
  matrix products  28.8 us (9%)
  local copies, waits for them, and re-layouts  15.6 us (5%)
    ppermute x12, starting transfers between devices, extended(): lax.ppermute(last, axis, up)  40.8 us
    ppermute x12, starting transfers between devices, extended(): lax.ppermute(leading, axis, [(b, a) for a, b in up])  34.4 us
    ppermute x6, waiting for transfers between devices, extended_2(): lax.ppermute(lax.slice_in_dim(block, block.shape[dim] - width, None, axis...  28.6 us
    all_to_all x3, starting transfers between devices, from_everyone(): lax.all_to_all(jnp.broadcast_to(shard[None], (peers, *shard.shape)), axis...  24.5 us
    all_to_all x3, waiting for transfers between devices, from_everyone(): lax.all_to_all(jnp.broadcast_to(shard[None], (peers, *shard.shape)), axis...  23.9 us
    ppermute x6, starting transfers between devices, extended_2(): lax.ppermute(lax.slice_in_dim(block, 0, width, axis=dim), axis, backward)  21.9 us
    all_to_all x3, starting transfers between devices, sent_and_summed(): lax.all_to_all(parts, axis, split_axis=0, concat_axis=0, tiled=True)  20.2 us
    dot_general x24, matrix products, spread_values(): lax.dot_general(spread, col_table, (((1,), (1,)), ((), ())), precision=la...  16.1 us
  transfers between devices with their start and end apart: 42, of which 14 were waited for; matrix products, arithmetic and copies ran while one was open for 15% of the time, Pallas kernels for 0%

commit v1 on v0

v1 whole, which is shorter than its diff:
```python
import functools

import jax
import jax.numpy as jnp
from jax import lax
from jax.experimental import pallas as pl
from jax.experimental.pallas import tpu as pltpu
from jax.sharding import PartitionSpec as P

STEPS = 3
DT = 0.2
MESH = pl.DeviceIdType.MESH
F32 = jnp.float32
BF16 = jnp.bfloat16
SYM = ((0, 3, 4), (3, 1, 5), (4, 5, 2))
HALF_ROWS = 8


def split_two(x):
    high = x.astype(BF16)
    return high, (x - high.astype(F32)).astype(BF16)


def dot_nn(a, b):
    return jnp.dot(a, b, preferred_element_type=F32)


def dot_nt(a, b):
    return lax.dot_general(a, b, (((1,), (1,)), ((), ())), preferred_element_type=F32)


def along_y(a, lane, width):
    after = jnp.where(lane < width - 1, pltpu.roll(a, width - 1, 1), 0.0)
    before = jnp.where(lane > 0, pltpu.roll(a, 1, 1), 0.0)
    return after - before


def updated_stress(sig, dz, dx, dy, elastic, cone):
    half = 0.5 * DT
    common = half * (dz[0] + dx[1] + dy[2])
    trial = [
        sig[0] + DT * dz[0] + common,
        sig[1] + DT * dx[1] + common,
        sig[2] + DT * dy[2] + common,
        sig[3] + half * (dx[0] + dz[1]),
        sig[4] + half * (dy[0] + dz[2]),
        sig[5] + half * (dy[1] + dx[2]),
    ]
    pressure = (trial[0] + trial[1] + trial[2]) * (1.0 / 3.0)
    dev = [trial[i] - pressure for i in range(3)]
    second = 0.5 * (dev[0] * dev[0] + dev[1] * dev[1] + dev[2] * dev[2]) + (
        trial[3] * trial[3] + trial[4] * trial[4] + trial[5] * trial[5]
    )
    shrink = 1.0 / (1.0 + 1.5 * jnp.sqrt(second))
    factor = jnp.where(elastic, 1.0, jnp.where(cone, shrink, 0.0))
    new = [dev[i] * factor + pressure for i in range(3)]
    return new + [trial[i] * factor for i in range(3, 6)]


def kernel(
    sizes,
    stress,
    velocity,
    density,
    flags,
    pile0,
    mass,
    jack,
    pair_elem,
    pair_cell,
    stress_out,
    velocity_out,
    pile_out,
    sig,
    vx,
    v0,
    scale,
    flg,
    sigp,
    spk,
    pbuf,
    rxp,
    cbuf,
    crx,
    pvw,
    massv,
    jackv,
    elemv,
    cellv,
    crow,
    prow,
    acol,
    arow,
    bcol,
    brow,
    thi,
    tlo,
    phi,
    plo,
    acc_s,
    acc_c,
    count_c,
    sbuf,
    sdep,
    sown,
    rx,
    rxn,
    nown,
    local_sem,
    init_send,
    init_recv,
    halo_send,
    halo_recv,
    dep_send,
    dep_recv,
    part_send,
    part_recv,
    num_send,
    num_recv,
    all_send,
    all_recv,
    win_send,
    win_recv,
):
    depth_count, plan_count, cz, cx, cy, tiles, pairs, chunk = sizes
    units = 3 * tiles
    slots = -(-units // plan_count)
    rows = cz * cx
    prows = brow.shape[0]
    block_rows = tiles // 2 * 8
    d = lax.axis_index("depth")
    p = lax.axis_index("plan")
    d_up = lax.rem(d + 1, depth_count)
    d_dn = lax.rem(d + depth_count - 1, depth_count)
    p_up = lax.rem(p + 1, plan_count)
    p_dn = lax.rem(p + plan_count - 1, plan_count)
    own = pl.ds(8, cx)

    def remote(src, dst, send, recv, dd, pp):
        return pltpu.make_async_remote_copy(
            src_ref=src,
            dst_ref=dst,
            send_sem=send,
            recv_sem=recv,
            device_id={"depth": dd, "plan": pp},
            device_id_type=MESH,
        )

    local = [
        (stress, sig.at[:, pl.ds(1, cz), own, :]),
        (velocity, v0),
        (density, scale),
        (flags, flg.at[pl.ds(1, cz)]),
        (pile0, pvw.at[0, 1]),
        (mass, massv),
        (jack, jackv),
        (pair_elem, elemv),
        (pair_cell, cellv),
    ]
    local = [
        pltpu.make_async_copy(src, dst, local_sem.at[i]) for i, (src, dst) in enumerate(local)
    ]
    for copy in local:
        copy.start()

    barrier = pltpu.get_barrier_semaphore()
    corners = ((d_dn, p_dn), (d_dn, p_up), (d_up, p_dn), (d_up, p_up))
    for dd, pp in ((d_dn, p), (d_up, p)) + corners:
        pl.semaphore_signal(
            barrier, inc=1, device_id={"depth": dd, "plan": pp}, device_id_type=MESH
        )

    def greet(k, unused):
        pl.semaphore_signal(
            barrier,
            inc=1,
            device_id={"depth": d, "plan": lax.rem(p + k, plan_count)},
            device_id_type=MESH,
        )
        return unused

    lax.fori_loop(1, plan_count, greet, 0)
    for i in (0, 3):
        local[i].wait()

    def pack_edges(z, unused):
        at = pl.ds(z, 1)
        for c in range(6):
            spk[0, c, at, :] = sig[c, z + 1, 8:9, :]
            spk[1, c, at, :] = sig[c, z + 1, cx + 7 : cx + 8, :]
        spk[0, 6, at, :] = flg[z + 1, 0:1, :].astype(F32)
        spk[1, 6, at, :] = flg[z + 1, cx - 1 : cx, :].astype(F32)
        return unused

    lax.fori_loop(0, cz, pack_edges, 0)
    pl.semaphore_wait(barrier, plan_count + 5)

    init = [
        remote(pile0, pvw.at[0, 0], init_send.at[0], init_recv.at[0], d_up, p),
        remote(pile0, pvw.at[0, 2], init_send.at[1], init_recv.at[1], d_dn, p),
        remote(
            stress.at[:, cz - 1], sig.at[:, 0, own, :], init_send.at[2], init_recv.at[2], d_up, p
        ),
        remote(
            stress.at[:, 0], sig.at[:, cz + 1, own, :], init_send.at[3], init_recv.at[3], d_dn, p
        ),
        remote(spk.at[0], sigp.at[1], init_send.at[4], init_recv.at[4], d, p_dn),
        remote(spk.at[1], sigp.at[0], init_send.at[5], init_recv.at[5], d, p_up),
        remote(flags.at[cz - 1], flg.at[0], init_send.at[6], init_recv.at[6], d_up, p),
        remote(flags.at[0], flg.at[cz + 1], init_send.at[7], init_recv.at[7], d_dn, p),
    ]
    for copy in init:
        copy.start()

    for i in (1, 2, 4, 5, 6, 7, 8):
        local[i].wait()

    def tables(i, unused):
        at = pl.ds(pl.multiple_of(i * chunk, chunk), chunk)
        cell = cellv[:, at]
        elem = elemv[:, at]
        live = cell >= 0
        c_row = jnp.where(live, cell // cy, -1)
        c_col = jnp.where(live, cell % cy, -1)
        block = elem // (tiles * 1024)
        inner = elem - block * (tiles * 1024)
        half_row = inner // 128
        p_row = block * block_rows + (half_row // 16) * 8 + half_row % 8
        p_col = (half_row // 8 % 2) * 128 + inner % 128
        p_row = jnp.where(live, p_row, -1)
        crow[:, at] = c_row
        prow[:, at] = p_row
        across = lax.broadcasted_iota(jnp.int32, (cy, chunk), 0)
        acol[:, at] = (across == c_col).astype(F32).astype(BF16)
        arow[:, at] = (across[:rows] == c_row).astype(F32).astype(BF16)
        wide = lax.broadcasted_iota(jnp.int32, (256, chunk), 0)
        bcol[:, at] = (wide == p_col).astype(F32).astype(BF16)
        brow[:, at] = (wide[:prows] == p_row).astype(F32).astype(BF16)
        return unused

    lax.fori_loop(0, pairs // chunk, tables, 0)

    def split_start(z, unused):
        for c in range(3):
            high, low = split_two(v0[c, z])
            at = pl.ds(pl.multiple_of(c * rows + z * cx, 16), cx)
            thi[at, :] = high
            tlo[at, :] = low
        scale[z] = DT / scale[z]
        return unused

    lax.fori_loop(0, cz, split_start, 0)
    def pile_terms(s):
        acc_s[...] = jnp.zeros_like(acc_s)

        def body(i, unused):
            at = pl.ds(pl.multiple_of(i * chunk, chunk), chunk)
            col = acol[:, at]
            picked = dot_nn(thi[...], col) + dot_nn(tlo[...], col)
            here = lax.broadcasted_iota(jnp.int32, (rows, chunk), 0) == crow[:, at]
            row = brow[:, at]
            high, low = [], []
            for c in range(3):
                value = jnp.sum(
                    jnp.where(here, picked[c * rows : (c + 1) * rows], 0.0), axis=0, keepdims=True
                )
                first, second = split_two(value)
                high.append(row * first)
                low.append(row * second)
            wide = bcol[:, at]
            acc_s[...] += dot_nt(jnp.concatenate(high, 0), wide) + dot_nt(
                jnp.concatenate(low, 0), wide
            )
            return unused

        lax.fori_loop(0, pairs // chunk, body, 0)
        for b in range(3):
            for c in range(3):
                for t in range(tiles):
                    r = c * prows + b * block_rows + t // 2 * 8
                    l = t % 2 * 128
                    value = acc_s[r : r + 8, l : l + 128]
                    if s == 0:
                        value = value - sbuf[0, b, units + t] * pvw[0, b, c * tiles + t]
                    sbuf[s, b, c * tiles + t] = value

    def cell_terms(s):
        acc_c[...] = jnp.zeros_like(acc_c)
        for b in range(3):
            for c in range(3):
                for a in range(tiles // 2):
                    u = c * tiles + 2 * a
                    r = c * prows + b * block_rows + a * 8
                    phi[r : r + 8, 0:128] = pvw[s, b, u]
                    phi[r : r + 8, 128:256] = pvw[s, b, u + 1]
        high, low = split_two(phi[...])
        plo[0] = high
        plo[1] = low

        def body(i, unused):
            at = pl.ds(pl.multiple_of(i * chunk, chunk), chunk)
            col = bcol[:, at]
            picked = dot_nn(plo[0], col) + dot_nn(plo[1], col)
            here = lax.broadcasted_iota(jnp.int32, (prows, chunk), 0) == prow[:, at]
            row = arow[:, at]
            high, low = [], []
            for c in range(3):
                value = jnp.sum(
                    jnp.where(here, picked[c * prows : (c + 1) * prows], 0.0),
                    axis=0,
                    keepdims=True,
                )
                first, second = split_two(value)
                high.append(row * first)
                low.append(row * second)
            wide = acol[:, at]
            acc_c[...] += dot_nt(jnp.concatenate(high, 0), wide) + dot_nt(
                jnp.concatenate(low, 0), wide
            )
            return unused

        lax.fori_loop(0, pairs // chunk, body, 0)

    count_c[...] = dot_nt(arow[...], acol[...])
    acc_s[0:prows, :] = dot_nt(brow[...], bcol[...])
    for b in range(3):
        for t in range(tiles):
            r = b * block_rows + t // 2 * 8
            l = t % 2 * 128
            sbuf[0, b, units + t] = acc_s[r : r + 8, l : l + 128]
    phi[...] = jnp.zeros_like(phi)
    init[0].wait_recv()
    init[1].wait_recv()

    def depth_leg(s):
        many = pl.ds(0, units + tiles if s == 0 else units)
        return [
            remote(
                sbuf.at[s, 0, many],
                sdep.at[s, 1, many],
                dep_send.at[s, 0],
                dep_recv.at[s, 0],
                d_dn,
                p,
            ),
            remote(
                sbuf.at[s, 2, many],
                sdep.at[s, 0, many],
                dep_send.at[s, 1],
                dep_recv.at[s, 1],
                d_up,
                p,
            ),
        ]

    def start_parts(s):
        many = units + tiles if s == 0 else units
        for u in range(many):
            sown[s, u] = sbuf[s, 1, u] + sdep[s, 0, u] + sdep[s, 1, u]

        def go(j, number):
            def body(k, unused):
                q = lax.rem(p + k, plan_count)
                u = q + plan_count * j

                def send():
                    if number:
                        remote(
                            sown.at[0, units + lax.rem(u, tiles)],
                            rxn.at[j, p],
                            num_send.at[j],
                            num_recv.at[j],
                            d,
                            q,
                        ).start()
                    else:
                        remote(
                            sown.at[s, u],
                            rx.at[s, j, p],
                            part_send.at[s, j],
                            part_recv.at[s, j],
                            d,
                            q,
                        ).start()

                if plan_count * (j + 1) <= units:
                    send()
                else:
                    pl.when(u < units)(send)
                return unused

            lax.fori_loop(1, plan_count, body, 0)

        for j in range(slots):
            go(j, False)
        if s == 0:
            for j in range(slots):
                go(j, True)

    def owners(j, work):
        if plan_count * (j + 1) <= units:
            work()
        else:
            pl.when(p + plan_count * j < units)(work)

    def total(get):
        value = get(0)
        for i in range(1, plan_count):
            value = value + get(i)
        return value

    def update_pile(s):
        for j in range(slots):
            u = p + plan_count * j

            def work():
                t = lax.rem(u, tiles)
                most = pl.ds(0, plan_count - 1)
                remote(
                    rx.at[s, j, most],
                    rx.at[s, j, most],
                    part_send.at[s, j],
                    part_recv.at[s, j],
                    d,
                    p_up,
                ).wait_recv()
                rx[s, j, p] = sown[s, u]
                if s == 0:
                    remote(
                        rxn.at[j, most],
                        rxn.at[j, most],
                        num_send.at[j],
                        num_recv.at[j],
                        d,
                        p_up,
                    ).wait_recv()
                    rxn[j, p] = sown[0, units + t]
                    nown[j] = total(lambda i: rxn[j, i])
                force = jackv[u] + total(lambda i: rx[s, j, i])
                before = pvw[s, 1, u]
                if s > 0:
                    force = force - nown[j] * before
                pvw[s + 1, 1, u] = before + DT * force / massv[t]

                def body(k, unused):
                    remote(
                        pvw.at[s + 1, 1, u],
                        pvw.at[s + 1, 1, u],
                        all_send.at[s, j],
                        all_recv.at[s, j],
                        d,
                        lax.rem(p + k, plan_count),
                    ).start()
                    return unused

                lax.fori_loop(1, plan_count, body, 0)

            owners(j, work)

    def wait_pile(s):
        for j in range(slots):
            here = min(plan_count, units - plan_count * j)

            def take(number):
                if number > 0:
                    some = pl.ds(0, number)
                    remote(
                        pvw.at[s + 1, 1, some],
                        pvw.at[s + 1, 1, some],
                        all_send.at[s, j],
                        all_recv.at[s, j],
                        d,
                        p_up,
                    ).wait_recv()

            if here == plan_count:
                take(here - 1)
            else:
                pl.when(p < here)(lambda: take(here - 1))
                pl.when(p >= here)(lambda: take(here))

    def window_leg(s):
        return [
            remote(
                pvw.at[s, 1], pvw.at[s, 0], win_send.at[s - 1, 0], win_recv.at[s - 1, 0], d_up, p
            ),
            remote(
                pvw.at[s, 1], pvw.at[s, 2], win_send.at[s - 1, 1], win_recv.at[s - 1, 1], d_dn, p
            ),
        ]

    lane = lax.broadcasted_iota(jnp.int32, (cx, cy), 1)
    lane_p = lax.broadcasted_iota(jnp.int32, (cz, cy), 1)

    def new_velocity(s):
        def body(z, unused):
            for c in (1, 3, 5):
                sig[c, z + 1, 7:8, :] = sigp[0, c, pl.ds(z, 1), :]
                sig[c, z + 1, cx + 8 : cx + 9, :] = sigp[1, c, pl.ds(z, 1), :]
            for c in range(3):
                i, j, k = SYM[c]
                force = sig[i, z + 2, own, :] - sig[i, z, own, :]
                force += sig[j, z + 1, pl.ds(9, cx), :] - sig[j, z + 1, pl.ds(7, cx), :]
                force += along_y(sig[k, z + 1, own, :], lane, cy)
                old = v0[c, z] if s == 0 else vx[s - 1, c, z + 2, own, :]
                at = pl.ds(pl.multiple_of(z * cx, 16), cx)
                spot = pl.ds(pl.multiple_of(c * rows + z * cx, 16), cx)
                push = acc_c[spot, :] - count_c[at, :] * old
                new = old + scale[z] * (0.5 * force + push)
                vx[s, c, z + 2, own, :] = new
                if s < STEPS - 1:
                    high, low = split_two(new)
                    thi[spot, :] = high
                    tlo[spot, :] = low
                row = pl.ds(z, 1)
                pbuf[s, 0, c, 0, row, :] = new[0:1]
                pbuf[s, 1, c, 1, row, :] = new[cx - 1 : cx]
                if s < STEPS - 1:
                    pbuf[s, 0, c, 1, row, :] = new[1:2]
                    pbuf[s, 1, c, 0, row, :] = new[cx - 2 : cx - 1]
            return unused

        lax.fori_loop(0, cz, body, 0)
        if s < STEPS - 1:
            for i in range(4):
                z = cz - 1 if i // 2 else 0
                x = cx - 1 if i % 2 else 0
                for c in range(3):
                    cbuf[s, i, c : c + 1, :] = vx[s, c, z + 2, 8 + x : 9 + x, :]

    def halo_leg(s):
        w = 2 if s < STEPS - 1 else 1
        xs0 = pl.ds(0, w)
        xs1 = pl.ds(2 - w, w)
        mid = pl.ds(8, cz)
        send = lambda i: (halo_send.at[s, i], halo_recv.at[s, i])
        copies = [
            remote(
                vx.at[s, :, pl.ds(cz + 2 - w, w), own, :],
                vx.at[s, :, pl.ds(2 - w, w), own, :],
                *send(0),
                d_up,
                p,
            ),
            remote(
                vx.at[s, :, pl.ds(2, w), own, :],
                vx.at[s, :, pl.ds(cz + 2, w), own, :],
                *send(1),
                d_dn,
                p,
            ),
            remote(pbuf.at[s, 0, :, xs0], rxp.at[s, 1, :, xs0, mid, :], *send(2), d, p_dn),
            remote(pbuf.at[s, 1, :, xs1], rxp.at[s, 0, :, xs1, mid, :], *send(3), d, p_up),
        ]
        if s < STEPS - 1:
            for i in range(4):
                copies.append(remote(cbuf.at[s, i], crx.at[s, i], *send(4 + i), *corners[i]))
        return copies

    def new_stress(s):
        last = s == STEPS - 1

        @pl.when(d == 0)
        def _():
            vx[s, :, 0:2, own, :] = jnp.zeros((3, 2, cx, cy), F32)
            if not last:
                crx[s, 2:4] = jnp.zeros((2, 3, cy), F32)

        @pl.when(d == depth_count - 1)
        def _():
            vx[s, :, cz + 2 : cz + 4, own, :] = jnp.zeros((3, 2, cx, cy), F32)
            if not last:
                crx[s, 0:2] = jnp.zeros((2, 3, cy), F32)

        @pl.when(p == 0)
        def _():
            rxp[s, 0, :, :, 8 : 8 + cz, :] = jnp.zeros((3, 2, cz, cy), F32)
            if not last:
                for i in (1, 3):
                    crx[s, i] = jnp.zeros((3, cy), F32)

        @pl.when(p == plan_count - 1)
        def _():
            rxp[s, 1, :, :, 8 : 8 + cz, :] = jnp.zeros((3, 2, cz, cy), F32)
            if not last:
                for i in (0, 2):
                    crx[s, i] = jnp.zeros((3, cy), F32)

        if not last:
            for c in range(3):
                for side in range(2):
                    x = 7 if side == 0 else cx + 8
                    below = crx[s, 3 - side, c : c + 1, :]
                    above = crx[s, 1 - side, c : c + 1, :]
                    vx[s, c, 1, x : x + 1, :] = below
                    vx[s, c, cz + 2, x : x + 1, :] = above
                    rxp[s, side, c, 1 - side, 7:8, :] = below
                    rxp[s, side, c, 1 - side, cz + 8 : cz + 9, :] = above

        def rows_in(z, unused):
            for c in range(3):
                vx[s, c, z + 2, 7:8, :] = rxp[s, 0, c, 1, pl.ds(z + 8, 1), :]
                vx[s, c, z + 2, cx + 8 : cx + 9, :] = rxp[s, 1, c, 0, pl.ds(z + 8, 1), :]
            return unused

        lax.fori_loop(0, cz, rows_in, 0)

        def body(layer, unused):
            dz = [
                vx[s, c, layer + 2, own, :] - vx[s, c, layer, own, :] for c in range(3)
            ]
            dx = [
                vx[s, c, layer + 1, pl.ds(9, cx), :] - vx[s, c, layer + 1, pl.ds(7, cx), :]
                for c in range(3)
            ]
            dy = [along_y(vx[s, c, layer + 1, own, :], lane, cy) for c in range(3)]
            flag = flg[layer]
            new = updated_stress(
                [sig[c, layer, own, :] for c in range(6)], dz, dx, dy, flag == 0, flag == 1
            )
            for c in range(6):
                sig[c, layer, own, :] = new[c]
            return unused

        if last:
            lax.fori_loop(1, cz + 1, body, 0)
            return
        lax.fori_loop(0, cz + 2, body, 0)
        for side in range(2):
            inner = [pbuf[s, side, c, side] for c in range(3)]
            outer = [rxp[s, side, c, side, 8 : 8 + cz, :] for c in range(3)]
            sign = 1.0 if side == 0 else -1.0
            ring = 1 - side
            dz = [
                rxp[s, side, c, ring, 9 : 9 + cz, :] - rxp[s, side, c, ring, 7 : 7 + cz, :]
                for c in range(3)
            ]
            dx = [sign * (inner[c] - outer[c]) for c in range(3)]
            dy = [along_y(rxp[s, side, c, ring, 8 : 8 + cz, :], lane_p, cy) for c in range(3)]
            flag = sigp[side, 6]
            new = updated_stress(
                [sigp[side, c] for c in range(6)], dz, dx, dy, flag == 0.0, flag == 1.0
            )
            for c in range(6):
                sigp[side, c] = new[c]
        clear_outside()

    def clear_outside():
        @pl.when(d == 0)
        def _():
            sig[:, 0, own, :] = jnp.zeros((6, cx, cy), F32)

        @pl.when(d == depth_count - 1)
        def _():
            sig[:, cz + 1, own, :] = jnp.zeros((6, cx, cy), F32)

        @pl.when(p == 0)
        def _():
            sigp[0, 0:6] = jnp.zeros((6, cz, cy), F32)

        @pl.when(p == plan_count - 1)
        def _():
            sigp[1, 0:6] = jnp.zeros((6, cz, cy), F32)

    def start(copies):
        for copy in copies:
            copy.start()
        return copies

    def arrive(copies):
        for copy in copies:
            copy.wait_recv()

    pile_terms(0)
    legs = [start(depth_leg(0))]
    cell_terms(0)
    arrive(legs[0])
    start_parts(0)
    arrive(init[2:])
    clear_outside()
    new_velocity(0)
    halos = [start(halo_leg(0))]
    pile_terms(1)
    legs.append(start(depth_leg(1)))
    update_pile(0)
    arrive(halos[0])
    new_stress(0)
    arrive(legs[1])
    start_parts(1)
    wait_pile(0)
    windows = [start(window_leg(1))]
    arrive(windows[0])
    cell_terms(1)
    new_velocity(1)
    halos.append(start(halo_leg(1)))
    pile_terms(2)
    legs.append(start(depth_leg(2)))
    update_pile(1)
    arrive(halos[1])
    new_stress(1)
    arrive(legs[2])
    start_parts(2)
    wait_pile(1)
    windows.append(start(window_leg(2)))
    arrive(windows[1])
    cell_terms(2)
    new_velocity(2)
    halos.append(start(halo_leg(2)))
    velocity_back = pltpu.make_async_copy(
        vx.at[2, :, pl.ds(2, cz), own, :], velocity_out, local_sem.at[0]
    )
    velocity_back.start()
    update_pile(2)
    arrive(halos[2])
    new_stress(2)
    stress_back = pltpu.make_async_copy(
        sig.at[:, pl.ds(1, cz), own, :], stress_out, local_sem.at[1]
    )
    stress_back.start()
    wait_pile(2)
    pile_back = pltpu.make_async_copy(pvw.at[3, 1], pile_out, local_sem.at[2])
    pile_back.start()

    for copies in [init] + halos + legs + windows:
        for copy in copies:
            copy.wait_send()
    for s in range(STEPS):
        for j in range(slots):
            here = min(plan_count, units - plan_count * j)

            def gone(number):
                if number > 0:
                    some = pl.ds(0, number)
                    remote(
                        rx.at[s, j, some],
                        rx.at[s, j, some],
                        part_send.at[s, j],
                        part_recv.at[s, j],
                        d,
                        p_up,
                    ).wait_send()
                    if s == 0:
                        remote(
                            rxn.at[j, some],
                            rxn.at[j, some],
                            num_send.at[j],
                            num_recv.at[j],
                            d,
                            p_up,
                        ).wait_send()

            if here == plan_count:
                gone(here - 1)
            else:
                pl.when(p < here)(lambda: gone(here - 1))
                pl.when(p >= here)(lambda: gone(here))

            def spread():
                most = pl.ds(0, plan_count - 1)
                remote(
                    rx.at[s, j, most],
                    rx.at[s, j, most],
                    all_send.at[s, j],
                    all_recv.at[s, j],
                    d,
                    p_up,
                ).wait_send()

            owners(j, spread)
    velocity_back.wait()
    stress_back.wait()
    pile_back.wait()


def shards(
    depth_count,
    plan_count,
    stress,
    velocity,
    density,
    flags,
    pile_velocity,
    pile_mass,
    jack_force,
    pair_elem,
    pair_cell,
):
    cz, cx, cy = density.shape
    width = pile_mass.shape[0]
    tiles = width // 1024
    pairs = pair_elem.shape[1]
    chunk = min(512, pairs)
    units = 3 * tiles
    slots = -(-units // plan_count)
    rows = cz * cx
    prows = -(-(3 * width // 256) // 16) * 16
    sizes = (depth_count, plan_count, cz, cx, cy, tiles, pairs, chunk)
    vm = lambda *shape: pltpu.VMEM(shape, F32)
    half = lambda *shape: pltpu.VMEM(shape, BF16)
    whole = lambda *shape: pltpu.VMEM(shape, jnp.int32)
    dma = lambda *shape: pltpu.SemaphoreType.DMA(shape)
    scratch = [
        vm(6, cz + 2, cx + 16, cy),
        vm(STEPS, 3, cz + 4, cx + 16, cy),
        vm(3, cz, cx, cy),
        vm(cz, cx, cy),
        whole(cz + 2, cx, cy),
        vm(2, 7, cz, cy),
        vm(2, 7, cz, cy),
        vm(STEPS, 2, 3, 2, cz, cy),
        vm(STEPS, 2, 3, 2, cz + 16, cy),
        vm(STEPS, 4, 3, cy),
        vm(STEPS, 4, 3, cy),
        vm(STEPS + 1, 3, units, 8, 128),
        vm(tiles, 8, 128),
        vm(units, 8, 128),
        whole(1, pairs),
        whole(1, pairs),
        whole(1, pairs),
        whole(1, pairs),
        half(cy, pairs),
        half(rows, pairs),
        half(256, pairs),
        half(prows, pairs),
        half(3 * rows, cy),
        half(3 * rows, cy),
        vm(3 * prows, 256),
        half(2, 3 * prows, 256),
        vm(3 * prows, 256),
        vm(3 * rows, cy),
        vm(rows, cy),
        vm(STEPS, 3, units + tiles, 8, 128),
        vm(STEPS, 2, units + tiles, 8, 128),
        vm(STEPS, units + tiles, 8, 128),
        vm(STEPS, slots, plan_count, 8, 128),
        vm(slots, plan_count, 8, 128),
        vm(slots, 8, 128),
        dma(9),
        dma(8),
        dma(8),
        dma(STEPS, 8),
        dma(STEPS, 8),
        dma(STEPS, 2),
        dma(STEPS, 2),
        dma(STEPS, slots),
        dma(STEPS, slots),
        dma(slots),
        dma(slots),
        dma(STEPS, slots),
        dma(STEPS, slots),
        dma(STEPS - 1, 2),
        dma(STEPS - 1, 2),
    ]
    anywhere = pl.BlockSpec(memory_space=pl.ANY)
    stress, velocity, pile = pl.pallas_call(
        functools.partial(kernel, sizes),
        out_shape=(
            jax.ShapeDtypeStruct(stress.shape, F32),
            jax.ShapeDtypeStruct(velocity.shape, F32),
            jax.ShapeDtypeStruct((units, 8, 128), F32),
        ),
        in_specs=[anywhere] * 9,
        out_specs=(anywhere,) * 3,
        scratch_shapes=scratch,
        compiler_params=pltpu.CompilerParams(
            collective_id=0, has_side_effects=True, vmem_limit_bytes=40 * 1024 * 1024
        ),
    )(
        stress,
        velocity,
        density,
        flags,
        pile_velocity.reshape(units, 8, 128),
        pile_mass.reshape(tiles, 8, 128),
        jack_force.reshape(units, 8, 128),
        pair_elem,
        pair_cell,
    )
    return stress, velocity, pile.reshape(3, width)


def solution(mesh):
    field = P(None, "depth", "plan", None)
    cells = P("depth", "plan", None)
    placed = (
        field,
        field,
        cells,
        cells,
        P(None, "depth"),
        P("depth"),
        P(None, "depth"),
        P("depth", "plan"),
        P("depth", "plan"),
    )
    return jax.shard_map(
        functools.partial(shards, mesh.shape["depth"], mesh.shape["plan"]),
        mesh=mesh,
        in_specs=placed,
        out_specs=(field, field, P(None, "depth")),
        check_vma=False,
    )
```

time: 312 us -> 84.4 us (0.27)
  the two profiles are of different devices: /device:TPU:256 before, /device:TPU:64 now
where the time goes in v1:
time: 84.4 us; the launch traced here: 84.1 us
  Pallas kernels  77 us (91%)
  local copies, waits for them, and re-layouts  6.39 us (8%)
    pallas_call x1, Pallas kernels, shards(): pl.pallas_call(functools.partial(kernel, sizes), out_shape=(jax.ShapeDtyp...  77 us
    unnamed x16, local copies, waits for them, and re-layouts  3.78 us

profile of v1, /device:TPU:64, one launch (start us, length us, event | category | flops | bytes accessed | tf_op | source)
XLA Modules:
  0.0 84.1 jit_solution(8763845848471127131)
XLA Ops:
  0.6 0.0 copy-start.2
  0.6 0.0 copy-start.3
  0.7 1.0 %reshape.18.pile0 = f32[18,8,128]{2,1,0:T(8,128)S(1)} reshape(f32[3,6144]{1,0:T(4,128)} %param.13) | data formatting | bytes 147456 | tf_op jit(solution)/shard_map/reshape | solution.py:873
  1.6 0.0 copy-start.4
  1.7 0.0 copy-start.5
  1.7 0.0 copy-start.6
  1.7 1.0 %reshape.20.jack = f32[18,8,128]{2,1,0:T(8,128)S(1)} reshape(f32[3,6144]{1,0:T(4,128)} %param.15) | data formatting | bytes 147456 | tf_op jit(solution)/shard_map/reshape | solution.py:875
  2.6 0.0 copy-done.2
  2.6 0.0 copy-done.3
  2.7 0.0 copy-done.4
  2.7 0.0 copy-done.5
  2.7 0.0 copy-done.6
  2.7 0.0 copy-start
  2.7 1.1 %copy-done = f32[6,8,16,256]{3,2,1,0:T(8,128)S(1)} copy-done((f32[6,8,16,256]{3,2,1,0:T(8,128)S(1)}, f32[6,8,16,256]{3,2,1,0:T(8,128)}, u32[]{:S(2)}) %copy-start) | copy-done | bytes 786456
  3.8 0.0 copy-start.1
  3.8 1.0 %copy-done.1 = f32[3,8,16,256]{3,2,1,0:T(8,128)S(1)} copy-done((f32[3,8,16,256]{3,2,1,0:T(8,128)S(1)}, f32[3,8,16,256]{3,2,1,0:T(8,128)}, u32[]{:S(2)}) %copy-start.1) | copy-done | bytes 393240
  4.8 77.0 %shard_map.112 = (f32[6,8,16,256]{3,2,1,0:T(8,128)S(1)}, f32[3,8,16,256]{3,2,1,0:T(8,128)S(1)}, f32[18,8,128]{2,1,0:T(8,128)S(1)}) custom-call(f32[6,8,16,256]{3,2,1,0:T(8,128)S(1)} %copy-done, f32[3,8,16,256]{3,2,1,0:T(8,128)S(1)} %copy-done.1, f32[8,16,256]{2,1,0:T(8,128)S(1)} %copy-done.2, s32[8,16,256]{2,1,0:T(8,128)S(1)} %copy-done.3, ...), custom_call_target="tpu_custom_call" | custom-call | tf_op jit(solution)/shard_map/pallas_call | solution.py:855
  81.8 0.7 reshape.21
  82.5 0.9 %copy.14 = f32[6,8,16,256]{3,2,1,0:T(8,128)} copy(f32[6,8,16,256]{3,2,1,0:T(8,128)S(1)} %get-tuple-element.12) | data formatting | bytes 1572864
  83.4 0.7 copy.15
Async XLA Ops:
  0.6 2.0 %copy-start.2 = (f32[8,16,256]{2,1,0:T(8,128)S(1)}, f32[8,16,256]{2,1,0:T(8,128)}, u32[]{:S(2)}) copy-start(f32[8,16,256]{2,1,0:T(8,128)} %density.1) | copy-start | bytes 393220
  0.6 2.0 %copy-start.3 = (s32[8,16,256]{2,1,0:T(8,128)S(1)}, s32[8,16,256]{2,1,0:T(8,128)}, u32[]{:S(2)}) copy-start(s32[8,16,256]{2,1,0:T(8,128)} %flags.1) | copy-start | bytes 393220
  1.6 1.0 %copy-start.4 = (f32[6144]{0:T(1024)S(1)}, f32[6144]{0:T(1024)}, u32[]{:S(2)}) copy-start(f32[6144]{0:T(1024)} %param.14) | copy-start | bytes 73732
  1.7 1.0 %copy-start.5 = (s32[1,2048]{1,0:T(1,128)S(1)}, s32[1,2048]{1,0:T(1,128)}, u32[]{:S(2)}) copy-start(s32[1,2048]{1,0:T(1,128)} %pair_elem.1) | copy-start | bytes 24580
  1.7 1.0 %copy-start.6 = (s32[1,2048]{1,0:T(1,128)S(1)}, s32[1,2048]{1,0:T(1,128)}, u32[]{:S(2)}) copy-start(s32[1,2048]{1,0:T(1,128)} %pair_cell.1) | copy-start | bytes 24580
  2.7 1.1 %copy-start = (f32[6,8,16,256]{3,2,1,0:T(8,128)S(1)}, f32[6,8,16,256]{3,2,1,0:T(8,128)}, u32[]{:S(2)}) copy-start(f32[6,8,16,256]{3,2,1,0:T(8,128)} %stress.1) | copy-start | bytes 2359300
  3.8 1.0 %copy-start.1 = (f32[3,8,16,256]{3,2,1,0:T(8,128)S(1)}, f32[3,8,16,256]{3,2,1,0:T(8,128)}, u32[]{:S(2)}) copy-start(f32[3,8,16,256]{3,2,1,0:T(8,128)} %velocity.1) | copy-start | bytes 1179652

commit v2 on v1

--- a/solution.py
+++ b/solution.py
@@ -85,6 +85,8 @@
     pvw,
     massv,
     jackv,
+    pilev,
+    jackw,
     elemv,
     cellv,
     crow,
@@ -101,9 +103,10 @@
     acc_c,
     count_c,
     sbuf,
-    sdep,
-    sown,
     rx,
+    nbuf,
+    ndep,
+    nsum,
     rxn,
     nown,
     local_sem,
@@ -119,8 +122,6 @@
     num_recv,
     all_send,
     all_recv,
-    win_send,
-    win_recv,
 ):
     depth_count, plan_count, cz, cx, cy, tiles, pairs, chunk = sizes
     units = 3 * tiles
@@ -135,6 +136,29 @@
     p_up = lax.rem(p + 1, plan_count)
     p_dn = lax.rem(p + plan_count - 1, plan_count)
     own = pl.ds(8, cx)
+    y_count = plan_count // 2
+    y = p // 2
+    z_low = p % 2
+    odd = d % 2
+    d_near = d + 1 - 2 * odd
+    d_far = lax.rem(d + depth_count - 1 + 2 * odd, depth_count)
+    kinds = ((d_far, 2 * odd), (d_near, 2 - 2 * odd), (d, 1))
+
+    def everyone(first, visit):
+        def body(i, unused):
+            step = (i + 1) // 2
+            yy = lax.rem(y + y_count // 2 + step * (1 - 2 * (i % 2)) + y_count, y_count)
+            for kind in range(first, 3):
+                dd, block = kinds[kind]
+                for z in (1 - z_low, z_low):
+                    act = functools.partial(visit, kind, dd, block, yy * 2 + z)
+                    if kind == 2 and z is z_low:
+                        pl.when(i < y_count - 1)(act)
+                    else:
+                        act()
+            return unused
+
+        lax.fori_loop(0, y_count, body, 0)
 
     def remote(src, dst, send, recv, dd, pp):
         return pltpu.make_async_remote_copy(
@@ -151,9 +175,9 @@
         (velocity, v0),
         (density, scale),
         (flags, flg.at[pl.ds(1, cz)]),
-        (pile0, pvw.at[0, 1]),
+        (pile0, pilev),
         (mass, massv),
-        (jack, jackv),
+        (jack, jackw),
         (pair_elem, elemv),
         (pair_cell, cellv),
     ]
@@ -165,21 +189,13 @@
 
     barrier = pltpu.get_barrier_semaphore()
     corners = ((d_dn, p_dn), (d_dn, p_up), (d_up, p_dn), (d_up, p_up))
-    for dd, pp in ((d_dn, p), (d_up, p)) + corners:
+
+    def greet(kind, dd, block, q):
         pl.semaphore_signal(
-            barrier, inc=1, device_id={"depth": dd, "plan": pp}, device_id_type=MESH
+            barrier, inc=1, device_id={"depth": dd, "plan": q}, device_id_type=MESH
         )
 
-    def greet(k, unused):
-        pl.semaphore_signal(
-            barrier,
-            inc=1,
-            device_id={"depth": d, "plan": lax.rem(p + k, plan_count)},
-            device_id_type=MESH,
-        )
-        return unused
-
-    lax.fori_loop(1, plan_count, greet, 0)
+    everyone(0, greet)
     for i in (0, 3):
         local[i].wait()
 
@@ -193,26 +209,21 @@
         return unused
 
     lax.fori_loop(0, cz, pack_edges, 0)
-    pl.semaphore_wait(barrier, plan_count + 5)
-
-    init = [
-        remote(pile0, pvw.at[0, 0], init_send.at[0], init_recv.at[0], d_up, p),
-        remote(pile0, pvw.at[0, 2], init_send.at[1], init_recv.at[1], d_dn, p),
-        remote(
-            stress.at[:, cz - 1], sig.at[:, 0, own, :], init_send.at[2], init_recv.at[2], d_up, p
-        ),
-        remote(
-            stress.at[:, 0], sig.at[:, cz + 1, own, :], init_send.at[3], init_recv.at[3], d_dn, p
-        ),
-        remote(spk.at[0], sigp.at[1], init_send.at[4], init_recv.at[4], d, p_dn),
-        remote(spk.at[1], sigp.at[0], init_send.at[5], init_recv.at[5], d, p_up),
-        remote(flags.at[cz - 1], flg.at[0], init_send.at[6], init_recv.at[6], d_up, p),
-        remote(flags.at[0], flg.at[cz + 1], init_send.at[7], init_recv.at[7], d_dn, p),
-    ]
-    for copy in init:
-        copy.start()
-
-    for i in (1, 2, 4, 5, 6, 7, 8):
+
+    local[4].wait()
+    local[6].wait()
+
+    def pile_tiles(t, unused):
+        for r in range(8):
+            at = pl.ds(pl.multiple_of(t * 1024 + r * 128, 128), 128)
+            for source, target, first in ((pilev, pvw.at[0], units), (jackw, jackv, 0)):
+                value = source[:, at]
+                for c in range(3):
+                    target[first + c * tiles + t, r : r + 1, :] = value[c : c + 1]
+        return unused
+
+    lax.fori_loop(0, tiles, pile_tiles, 0)
+    for i in (1, 2, 5, 7, 8):
         local[i].wait()
 
     def tables(i, unused):
@@ -279,20 +290,17 @@
                 for t in range(tiles):
                     r = c * prows + b * block_rows + t // 2 * 8
                     l = t % 2 * 128
-                    value = acc_s[r : r + 8, l : l + 128]
-                    if s == 0:
-                        value = value - sbuf[0, b, units + t] * pvw[0, b, c * tiles + t]
-                    sbuf[s, b, c * tiles + t] = value
+                    sbuf[s, b, c * tiles + t] = acc_s[r : r + 8, l : l + 128]
 
     def cell_terms(s):
         acc_c[...] = jnp.zeros_like(acc_c)
         for b in range(3):
             for c in range(3):
                 for a in range(tiles // 2):
-                    u = c * tiles + 2 * a
+                    u = b * units + c * tiles + 2 * a
                     r = c * prows + b * block_rows + a * 8
-                    phi[r : r + 8, 0:128] = pvw[s, b, u]
-                    phi[r : r + 8, 128:256] = pvw[s, b, u + 1]
+                    phi[r : r + 8, 0:128] = pvw[s, u]
+                    phi[r : r + 8, 128:256] = pvw[s, u + 1]
         high, low = split_two(phi[...])
         plo[0] = high
         plo[1] = low
@@ -327,167 +335,157 @@
         for t in range(tiles):
             r = b * block_rows + t // 2 * 8
             l = t % 2 * 128
-            sbuf[0, b, units + t] = acc_s[r : r + 8, l : l + 128]
+            nbuf[b, t] = acc_s[r : r + 8, l : l + 128]
     phi[...] = jnp.zeros_like(phi)
-    init[0].wait_recv()
-    init[1].wait_recv()
-
-    def depth_leg(s):
-        many = pl.ds(0, units + tiles if s == 0 else units)
-        return [
-            remote(
-                sbuf.at[s, 0, many],
-                sdep.at[s, 1, many],
-                dep_send.at[s, 0],
-                dep_recv.at[s, 0],
-                d_dn,
-                p,
-            ),
-            remote(
-                sbuf.at[s, 2, many],
-                sdep.at[s, 0, many],
-                dep_send.at[s, 1],
-                dep_recv.at[s, 1],
-                d_up,
-                p,
-            ),
-        ]
-
-    def start_parts(s):
-        many = units + tiles if s == 0 else units
-        for u in range(many):
-            sown[s, u] = sbuf[s, 1, u] + sdep[s, 0, u] + sdep[s, 1, u]
-
-        def go(j, number):
-            def body(k, unused):
-                q = lax.rem(p + k, plan_count)
-                u = q + plan_count * j
-
-                def send():
-                    if number:
-                        remote(
-                            sown.at[0, units + lax.rem(u, tiles)],
-                            rxn.at[j, p],
-                            num_send.at[j],
-                            num_recv.at[j],
-                            d,
-                            q,
-                        ).start()
-                    else:
-                        remote(
-                            sown.at[s, u],
-                            rx.at[s, j, p],
-                            part_send.at[s, j],
-                            part_recv.at[s, j],
-                            d,
-                            q,
-                        ).start()
-
-                if plan_count * (j + 1) <= units:
-                    send()
-                else:
-                    pl.when(u < units)(send)
-                return unused
-
-            lax.fori_loop(1, plan_count, body, 0)
-
-        for j in range(slots):
-            go(j, False)
-        if s == 0:
-            for j in range(slots):
-                go(j, True)
-
-    def owners(j, work):
+    pl.semaphore_wait(barrier, 3 * plan_count - 1)
+    mine = pl.ds(units, units)
+    init = [
+        remote(
+            nbuf.at[0], ndep.at[1], dep_send.at[0], dep_recv.at[0], d_dn, p
+        ),
+        remote(
+            nbuf.at[2], ndep.at[0], dep_send.at[1], dep_recv.at[1], d_up, p
+        ),
+        remote(
+            pvw.at[0, mine],
+            pvw.at[0, pl.ds(0, units)],
+            init_send.at[0],
+            init_recv.at[0],
+            d_up,
+            p,
+        ),
+        remote(
+            pvw.at[0, mine],
+            pvw.at[0, pl.ds(2 * units, units)],
+            init_send.at[1],
+            init_recv.at[1],
+            d_dn,
+            p,
+        ),
+        remote(
+            stress.at[:, cz - 1], sig.at[:, 0, own, :], init_send.at[2], init_recv.at[2], d_up, p
+        ),
+        remote(
+            stress.at[:, 0], sig.at[:, cz + 1, own, :], init_send.at[3], init_recv.at[3], d_dn, p
+        ),
+        remote(spk.at[0], sigp.at[1], init_send.at[4], init_recv.at[4], d, p_dn),
+        remote(spk.at[1], sigp.at[0], init_send.at[5], init_recv.at[5], d, p_up),
+        remote(flags.at[cz - 1], flg.at[0], init_send.at[6], init_recv.at[6], d_up, p),
+        remote(flags.at[0], flg.at[cz + 1], init_send.at[7], init_recv.at[7], d_dn, p),
+    ]
+    for copy in init:
+        copy.start()
+
+    def owned(j, q, work):
         if plan_count * (j + 1) <= units:
             work()
         else:
-            pl.when(p + plan_count * j < units)(work)
-
-    def total(get):
-        value = get(0)
-        for i in range(1, plan_count):
-            value = value + get(i)
-        return value
-
-    def update_pile(s):
-        for j in range(slots):
-            u = p + plan_count * j
-
-            def work():
-                t = lax.rem(u, tiles)
-                most = pl.ds(0, plan_count - 1)
-                remote(
-                    rx.at[s, j, most],
-                    rx.at[s, j, most],
-                    part_send.at[s, j],
-                    part_recv.at[s, j],
-                    d,
-                    p_up,
-                ).wait_recv()
-                rx[s, j, p] = sown[s, u]
-                if s == 0:
-                    remote(
-                        rxn.at[j, most],
-                        rxn.at[j, most],
+            pl.when(q + plan_count * j < units)(work)
+
+    def start_parts(s):
+        def visit(kind, dd, block, q):
+            for j in range(slots):
+                owned(
+                    j,
+                    q,
+                    lambda: remote(
+                        sbuf.at[s, block, q + plan_count * j],
+                        rx.at[s, j, kind * plan_count + p],
+                        part_send.at[s, j],
+                        part_recv.at[s, j],
+                        dd,
+                        q,
+                    ).start(),
+                )
+
+        everyone(0, visit)
+
+    def start_numbers():
+        for t in range(tiles):
+            nsum[t] = nbuf[1, t] + ndep[0, t] + ndep[1, t]
+
+        def visit(kind, dd, block, q):
+            for j in range(slots):
+                owned(
+                    j,
+                    q,
+                    lambda: remote(
+                        nsum.at[lax.rem(q + plan_count * j, tiles)],
+                        rxn.at[j, p],
                         num_send.at[j],
                         num_recv.at[j],
                         d,
-                        p_up,
-                    ).wait_recv()
-                    rxn[j, p] = sown[0, units + t]
-                    nown[j] = total(lambda i: rxn[j, i])
-                force = jackv[u] + total(lambda i: rx[s, j, i])
-                before = pvw[s, 1, u]
-                if s > 0:
-                    force = force - nown[j] * before
-                pvw[s + 1, 1, u] = before + DT * force / massv[t]
-
-                def body(k, unused):
+                        q,
+                    ).start(),
+                )
+
+        everyone(2, visit)
+
+    def some_of(ref, number, send, recv):
+        some = ref.at[pl.ds(0, number)]
+        return remote(some, some, send, recv, d, p_up)
+
+    def parts_wait(s, j, number):
+        return some_of(rx.at[s, j], number, part_send.at[s, j], part_recv.at[s, j])
+
+    def numbers_wait(j, number):
+        return some_of(rxn.at[j], number, num_send.at[j], num_recv.at[j])
+
+    def all_wait(s, j, number):
+        return some_of(pvw.at[s + 1], number, all_send.at[s, j], all_recv.at[s, j])
+
+    def not_mine(j, many, act):
+        here = min(plan_count, units - plan_count * j)
+        if here == plan_count:
+            act(here * many - 1)
+        else:
+            if here * many > 1:
+                pl.when(p < here)(lambda: act(here * many - 1))
+            pl.when(p >= here)(lambda: act(here * many))
+
+    def update_pile(s):
+        first = 0 if s < STEPS - 1 else 2
+        for j in range(slots):
+            u = p + plan_count * j
+
+            def work():
+                t = lax.rem(u, tiles)
+                parts_wait(s, j, 3 * plan_count - 1).wait_recv()
+                rx[s, j, 2 * plan_count + p] = sbuf[s, 1, u]
+                if s == 0:
+                    numbers_wait(j, plan_count - 1).wait_recv()
+                    rxn[j, p] = nsum[t]
+                    nown[j] = jnp.sum(rxn[j], axis=0)
+                before = pvw[s, units + u]
+                force = jackv[u] + jnp.sum(rx[s, j], axis=0) - nown[j] * before
+                pvw[s + 1, units + u] = before + DT * force / massv[t]
+
+                def visit(kind, dd, block, q):
                     remote(
-                        pvw.at[s + 1, 1, u],
-                        pvw.at[s + 1, 1, u],
+                        pvw.at[s + 1, units + u],
+                        pvw.at[s + 1, (2 - block) * units + u],
                         all_send.at[s, j],
                         all_recv.at[s, j],
-                        d,
-                        lax.rem(p + k, plan_count),
+                        dd,
+                        q,
                     ).start()
-                    return unused
-
-                lax.fori_loop(1, plan_count, body, 0)
-
-            owners(j, work)
+
+                everyone(first, visit)
+
+            owned(j, p, work)
 
     def wait_pile(s):
+        many = 3 if s < STEPS - 1 else 1
         for j in range(slots):
-            here = min(plan_count, units - plan_count * j)
-
-            def take(number):
-                if number > 0:
-                    some = pl.ds(0, number)
-                    remote(
-                        pvw.at[s + 1, 1, some],
-                        pvw.at[s + 1, 1, some],
-                        all_send.at[s, j],
-                        all_recv.at[s, j],
-                        d,
-                        p_up,
-                    ).wait_recv()
-
-            if here == plan_count:
-                take(here - 1)
-            else:
-                pl.when(p < here)(lambda: take(here - 1))
-                pl.when(p >= here)(lambda: take(here))
-
-    def window_leg(s):
-        return [
-            remote(
-                pvw.at[s, 1], pvw.at[s, 0], win_send.at[s - 1, 0], win_recv.at[s - 1, 0], d_up, p
-            ),
-            remote(
-                pvw.at[s, 1], pvw.at[s, 2], win_send.at[s - 1, 1], win_recv.at[s - 1, 1], d_dn, p
-            ),
-        ]
+            not_mine(j, many, lambda number: all_wait(s, j, number).wait_recv())
+
+    def drain_pile(s):
+        many = 3 if s < STEPS - 1 else 1
+        for j in range(slots):
+            not_mine(j, 3, lambda number: parts_wait(s, j, number).wait_send())
+            if s == 0:
+                not_mine(j, 1, lambda number: numbers_wait(j, number).wait_send())
+            owned(j, p, lambda: all_wait(s, j, many * plan_count - 1).wait_send())
 
     lane = lax.broadcasted_iota(jnp.int32, (cx, cy), 1)
     lane_p = lax.broadcasted_iota(jnp.int32, (cz, cy), 1)
@@ -672,37 +670,30 @@
             copy.wait_recv()
 
     pile_terms(0)
-    legs = [start(depth_leg(0))]
+    start_parts(0)
+    arrive(init[0:2])
+    start_numbers()
+    arrive(init[2:4])
     cell_terms(0)
-    arrive(legs[0])
-    start_parts(0)
-    arrive(init[2:])
+    arrive(init[4:])
     clear_outside()
     new_velocity(0)
     halos = [start(halo_leg(0))]
     pile_terms(1)
-    legs.append(start(depth_leg(1)))
+    start_parts(1)
     update_pile(0)
     arrive(halos[0])
     new_stress(0)
-    arrive(legs[1])
-    start_parts(1)
     wait_pile(0)
-    windows = [start(window_leg(1))]
-    arrive(windows[0])
     cell_terms(1)
+    update_pile(1)
     new_velocity(1)
     halos.append(start(halo_leg(1)))
     pile_terms(2)
-    legs.append(start(depth_leg(2)))
-    update_pile(1)
+    start_parts(2)
     arrive(halos[1])
     new_stress(1)
-    arrive(legs[2])
-    start_parts(2)
     wait_pile(1)
-    windows.append(start(window_leg(2)))
-    arrive(windows[1])
     cell_terms(2)
     new_velocity(2)
     halos.append(start(halo_leg(2)))
@@ -718,55 +709,23 @@
     )
     stress_back.start()
     wait_pile(2)
-    pile_back = pltpu.make_async_copy(pvw.at[3, 1], pile_out, local_sem.at[2])
+
+    def pile_lines(t, unused):
+        for r in range(8):
+            at = pl.ds(pl.multiple_of(t * 1024 + r * 128, 128), 128)
+            for c in range(3):
+                pilev[c : c + 1, at] = pvw[STEPS, units + c * tiles + t, r : r + 1, :]
+        return unused
+
+    lax.fori_loop(0, tiles, pile_lines, 0)
+    pile_back = pltpu.make_async_copy(pilev, pile_out, local_sem.at[2])
     pile_back.start()
 
-    for copies in [init] + halos + legs + windows:
+    for copies in [init] + halos:
         for copy in copies:
             copy.wait_send()
     for s in range(STEPS):
-        for j in range(slots):
-            here = min(plan_count, units - plan_count * j)
-
-            def gone(number):
-                if number > 0:
-                    some = pl.ds(0, number)
-                    remote(
-                        rx.at[s, j, some],
-                        rx.at[s, j, some],
-                        part_send.at[s, j],
-                        part_recv.at[s, j],
-                        d,
-                        p_up,
-                    ).wait_send()
-                    if s == 0:
-                        remote(
-                            rxn.at[j, some],
-                            rxn.at[j, some],
-                            num_send.at[j],
-                            num_recv.at[j],
-                            d,
-                            p_up,
-                        ).wait_send()
-
-            if here == plan_count:
-                gone(here - 1)
-            else:
-                pl.when(p < here)(lambda: gone(here - 1))
-                pl.when(p >= here)(lambda: gone(here))
-
-            def spread():
-                most = pl.ds(0, plan_count - 1)
-                remote(
-                    rx.at[s, j, most],
-                    rx.at[s, j, most],
-                    all_send.at[s, j],
-                    all_recv.at[s, j],
-                    d,
-                    p_up,
-                ).wait_send()
-
-            owners(j, spread)
+        drain_pile(s)
     velocity_back.wait()
     stress_back.wait()
     pile_back.wait()
@@ -811,9 +770,11 @@
         vm(STEPS, 2, 3, 2, cz + 16, cy),
         vm(STEPS, 4, 3, cy),
         vm(STEPS, 4, 3, cy),
-        vm(STEPS + 1, 3, units, 8, 128),
+        vm(STEPS + 1, 3 * units, 8, 128),
         vm(tiles, 8, 128),
         vm(units, 8, 128),
+        vm(3, width),
+        vm(3, width),
         whole(1, pairs),
         whole(1, pairs),
         whole(1, pairs),
@@ -829,10 +790,11 @@
         vm(3 * prows, 256),
         vm(3 * rows, cy),
         vm(rows, cy),
-        vm(STEPS, 3, units + tiles, 8, 128),
-        vm(STEPS, 2, units + tiles, 8, 128),
-        vm(STEPS, units + tiles, 8, 128),
-        vm(STEPS, slots, plan_count, 8, 128),
+        vm(STEPS, 3, units, 8, 128),
+        vm(STEPS, slots, 3 * plan_count, 8, 128),
+        vm(3, tiles, 8, 128),
+        vm(2, tiles, 8, 128),
+        vm(tiles, 8, 128),
         vm(slots, plan_count, 8, 128),
         vm(slots, 8, 128),
         dma(9),
@@ -840,16 +802,14 @@
         dma(8),
         dma(STEPS, 8),
         dma(STEPS, 8),
-        dma(STEPS, 2),
-        dma(STEPS, 2),
+        dma(2),
+        dma(2),
         dma(STEPS, slots),
         dma(STEPS, slots),
         dma(slots),
         dma(slots),
         dma(STEPS, slots),
         dma(STEPS, slots),
-        dma(STEPS - 1, 2),
-        dma(STEPS - 1, 2),
     ]
     anywhere = pl.BlockSpec(memory_space=pl.ANY)
     stress, velocity, pile = pl.pallas_call(
@@ -857,26 +817,26 @@
         out_shape=(
             jax.ShapeDtypeStruct(stress.shape, F32),
             jax.ShapeDtypeStruct(velocity.shape, F32),
-            jax.ShapeDtypeStruct((units, 8, 128), F32),
+            jax.ShapeDtypeStruct((3, width), F32),
         ),
         in_specs=[anywhere] * 9,
         out_specs=(anywhere,) * 3,
         scratch_shapes=scratch,
         compiler_params=pltpu.CompilerParams(
-            collective_id=0, has_side_effects=True, vmem_limit_bytes=40 * 1024 * 1024
+            collective_id=0, has_side_effects=True, vmem_limit_bytes=60 * 1024 * 1024
         ),
     )(
         stress,
         velocity,
         density,
         flags,
-        pile_velocity.reshape(units, 8, 128),
+        pile_velocity,
         pile_mass.reshape(tiles, 8, 128),
-        jack_force.reshape(units, 8, 128),
+        jack_force,
         pair_elem,
         pair_cell,
     )
-    return stress, velocity, pile.reshape(3, width)
+    return stress, velocity, pile
 
 
 def solution(mesh):

time: 84.4 us -> 89.6 us (1.062)
  the two profiles are of different devices: /device:TPU:64 before, /device:TPU:8 now
where the time goes in v2:
time: 89.6 us; the launch traced here: 89.4 us
  Pallas kernels  85 us (95%)
  local copies, waits for them, and re-layouts  3.75 us (4%)
    pallas_call x1, Pallas kernels, shards(): pl.pallas_call(functools.partial(kernel, sizes), out_shape=(jax.ShapeDtyp...  85 us
    unnamed x7, local copies, waits for them, and re-layouts  3.75 us

profile of v2, /device:TPU:8, one launch (start us, length us, event | category | flops | bytes accessed | tf_op | source)
XLA Modules:
  0.0 89.4 jit_solution(18024931648144470988)
XLA Ops:
  0.6 85.0 %shard_map.112 = (f32[6,8,16,256]{3,2,1,0:T(8,128)}, f32[3,8,16,256]{3,2,1,0:T(8,128)}, f32[3,6144]{1,0:T(4,128)}) custom-call(f32[6,8,16,256]{3,2,1,0:T(8,128)} %stress.1, f32[3,8,16,256]{3,2,1,0:T(8,128)} %velocity.1, f32[8,16,256]{2,1,0:T(8,128)} %density.1, s32[8,16,256]{2,1,0:T(8,128)} %flags.1, f32[3,6144]{1,0:T(4,128)} %pile0.1, ...), custom_call_target="tpu_custom_call" | custom-call | tf_op jit(solution)/shard_map/pallas_call | solution.py:815
  85.7 0.0 copy-start
  85.7 2.1 %copy.15 = f32[6,8,16,256]{3,2,1,0:T(8,128)} copy(f32[6,8,16,256]{3,2,1,0:T(8,128)} %get-tuple-element.6) | data formatting | bytes 1572864
  87.8 0.0 copy-done
  87.8 0.0 copy-start.1
  87.8 0.7 copy.16
  88.6 0.2 copy-done.1
  88.8 0.6 copy.17
Async XLA Ops:
  85.7 2.2 %copy-start = (f32[3,8,16,256]{3,2,1,0:T(8,128)S(1)}, f32[3,8,16,256]{3,2,1,0:T(8,128)}, u32[]{:S(2)}) copy-start(f32[3,8,16,256]{3,2,1,0:T(8,128)} %get-tuple-element.7) | copy-start | bytes 1179652
  87.8 1.0 %copy-start.1 = (f32[3,6144]{1,0:T(4,128)S(1)}, f32[3,6144]{1,0:T(4,128)}, u32[]{:S(2)}) copy-start(f32[3,6144]{1,0:T(4,128)} %get-tuple-element.8) | copy-start | bytes 221188

commit v3 on v2

--- a/solution.py
+++ b/solution.py
@@ -13,7 +13,8 @@
 F32 = jnp.float32
 BF16 = jnp.bfloat16
 SYM = ((0, 3, 4), (3, 1, 5), (4, 5, 2))
-HALF_ROWS = 8
+SUMS_IN_TWO = (0, 1, 2)
+TILES_IN_TWO = (0, 1)
 
 
 def split_two(x):
@@ -103,6 +104,8 @@
     acc_c,
     count_c,
     sbuf,
+    sdep,
+    sown,
     rx,
     nbuf,
     ndep,
@@ -122,6 +125,10 @@
     num_recv,
     all_send,
     all_recv,
+    leg_send,
+    leg_recv,
+    win_send,
+    win_recv,
 ):
     depth_count, plan_count, cz, cx, cy, tiles, pairs, chunk = sizes
     units = 3 * tiles
@@ -284,7 +291,7 @@
             )
             return unused
 
-        lax.fori_loop(0, pairs // chunk, body, 0)
+        lax.fori_loop(0, pairs // chunk, body, 0, unroll=True)
         for b in range(3):
             for c in range(3):
                 for t in range(tiles):
@@ -293,7 +300,6 @@
                     sbuf[s, b, c * tiles + t] = acc_s[r : r + 8, l : l + 128]
 
     def cell_terms(s):
-        acc_c[...] = jnp.zeros_like(acc_c)
         for b in range(3):
             for c in range(3):
                 for a in range(tiles // 2):
@@ -305,29 +311,20 @@
         plo[0] = high
         plo[1] = low
 
-        def body(i, unused):
-            at = pl.ds(pl.multiple_of(i * chunk, chunk), chunk)
-            col = bcol[:, at]
-            picked = dot_nn(plo[0], col) + dot_nn(plo[1], col)
-            here = lax.broadcasted_iota(jnp.int32, (prows, chunk), 0) == prow[:, at]
-            row = arow[:, at]
-            high, low = [], []
-            for c in range(3):
-                value = jnp.sum(
-                    jnp.where(here, picked[c * prows : (c + 1) * prows], 0.0),
-                    axis=0,
-                    keepdims=True,
-                )
-                first, second = split_two(value)
-                high.append(row * first)
-                low.append(row * second)
-            wide = acol[:, at]
-            acc_c[...] += dot_nt(jnp.concatenate(high, 0), wide) + dot_nt(
-                jnp.concatenate(low, 0), wide
+        picked = dot_nn(plo[0], bcol[...]) + dot_nn(plo[1], bcol[...])
+        here = lax.broadcasted_iota(jnp.int32, (prows, pairs), 0) == prow[...]
+        high, low = [], []
+        for c in range(3):
+            value = jnp.sum(
+                jnp.where(here, picked[c * prows : (c + 1) * prows], 0.0), axis=0, keepdims=True
             )
-            return unused
-
-        lax.fori_loop(0, pairs // chunk, body, 0)
+            first, second = split_two(value)
+            high.append(arow[...] * first)
+            low.append(arow[...] * second)
+        acc_c[...] = dot_nt(jnp.concatenate(high, 0), acol[...]) + dot_nt(
+            jnp.concatenate(low, 0), acol[...]
+        )
+
 
     count_c[...] = dot_nt(arow[...], acol[...])
     acc_s[0:prows, :] = dot_nt(brow[...], bcol[...])
@@ -337,6 +334,7 @@
             l = t % 2 * 128
             nbuf[b, t] = acc_s[r : r + 8, l : l + 128]
     phi[...] = jnp.zeros_like(phi)
+    pile_terms(0)
     pl.semaphore_wait(barrier, 3 * plan_count - 1)
     mine = pl.ds(units, units)
     init = [
@@ -373,8 +371,19 @@
         remote(flags.at[cz - 1], flg.at[0], init_send.at[6], init_recv.at[6], d_up, p),
         remote(flags.at[0], flg.at[cz + 1], init_send.at[7], init_recv.at[7], d_dn, p),
     ]
-    for copy in init:
-        copy.start()
+
+    def depth_leg(s):
+        return [
+            remote(sbuf.at[s, 0], sdep.at[s, 1], leg_send.at[s, 0], leg_recv.at[s, 0], d_dn, p),
+            remote(sbuf.at[s, 2], sdep.at[s, 0], leg_send.at[s, 1], leg_recv.at[s, 1], d_up, p),
+        ]
+
+    def window_leg(s):
+        block = lambda b: pvw.at[s + 1, pl.ds(b * units, units)]
+        return [
+            remote(block(1), block(0), win_send.at[s, 0], win_recv.at[s, 0], d_up, p),
+            remote(block(1), block(2), win_send.at[s, 1], win_recv.at[s, 1], d_dn, p),
+        ]
 
     def owned(j, q, work):
         if plan_count * (j + 1) <= units:
@@ -382,14 +391,16 @@
         else:
             pl.when(q + plan_count * j < units)(work)
 
-    def start_parts(s):
+    def send_parts(s):
         def visit(kind, dd, block, q):
             for j in range(slots):
+                u = q + plan_count * j
+                source = sown.at[s, u] if s in SUMS_IN_TWO else sbuf.at[s, block, u]
                 owned(
                     j,
                     q,
                     lambda: remote(
-                        sbuf.at[s, block, q + plan_count * j],
+                        source,
                         rx.at[s, j, kind * plan_count + p],
                         part_send.at[s, j],
                         part_recv.at[s, j],
@@ -398,7 +409,22 @@
                     ).start(),
                 )
 
-        everyone(0, visit)
+        everyone(2 if s in SUMS_IN_TWO else 0, visit)
+
+    def start_parts(s):
+        if s in SUMS_IN_TWO:
+            for copy in depth_leg(s):
+                copy.start()
+        else:
+            send_parts(s)
+
+    def middle_parts(s):
+        if s in SUMS_IN_TWO:
+            for copy in depth_leg(s):
+                copy.wait_recv()
+            for u in range(units):
+                sown[s, u] = sbuf[s, 1, u] + sdep[s, 0, u] + sdep[s, 1, u]
+            send_parts(s)
 
     def start_numbers():
         for t in range(tiles):
@@ -444,20 +470,21 @@
             pl.when(p >= here)(lambda: act(here * many))
 
     def update_pile(s):
-        first = 0 if s < STEPS - 1 else 2
+        first = 2 if s in TILES_IN_TWO or s == STEPS - 1 else 0
+        two = s in SUMS_IN_TWO
         for j in range(slots):
             u = p + plan_count * j
 
             def work():
                 t = lax.rem(u, tiles)
-                parts_wait(s, j, 3 * plan_count - 1).wait_recv()
-                rx[s, j, 2 * plan_count + p] = sbuf[s, 1, u]
+                parts_wait(s, j, (1 if two else 3) * plan_count - 1).wait_recv()
+                rx[s, j, 2 * plan_count + p] = sown[s, u] if two else sbuf[s, 1, u]
                 if s == 0:
                     numbers_wait(j, plan_count - 1).wait_recv()
                     rxn[j, p] = nsum[t]
                     nown[j] = jnp.sum(rxn[j], axis=0)
                 before = pvw[s, units + u]
-                force = jackv[u] + jnp.sum(rx[s, j], axis=0) - nown[j] * before
+                force = jackv[u] + jnp.sum(rx[s, j, (2 * plan_count if two else 0) :], axis=0) - nown[j] * before
                 pvw[s + 1, units + u] = before + DT * force / massv[t]
 
                 def visit(kind, dd, block, q):
@@ -474,15 +501,33 @@
 
             owned(j, p, work)
 
+    def own_pile(s):
+        if s in TILES_IN_TWO:
+            for j in range(slots):
+                not_mine(j, 1, lambda number: all_wait(s, j, number).wait_recv())
+            for copy in window_leg(s):
+                copy.start()
+
     def wait_pile(s):
+        if s in TILES_IN_TWO:
+            for copy in window_leg(s):
+                copy.wait_recv()
+            return
         many = 3 if s < STEPS - 1 else 1
         for j in range(slots):
             not_mine(j, many, lambda number: all_wait(s, j, number).wait_recv())
 
     def drain_pile(s):
-        many = 3 if s < STEPS - 1 else 1
+        many = 1 if s in TILES_IN_TWO or s == STEPS - 1 else 3
+        sums = 1 if s in SUMS_IN_TWO else 3
+        if s in SUMS_IN_TWO:
+            for copy in depth_leg(s):
+                copy.wait_send()
+        if s in TILES_IN_TWO:
+            for copy in window_leg(s):
+                copy.wait_send()
         for j in range(slots):
-            not_mine(j, 3, lambda number: parts_wait(s, j, number).wait_send())
+            not_mine(j, sums, lambda number: parts_wait(s, j, number).wait_send())
             if s == 0:
                 not_mine(j, 1, lambda number: numbers_wait(j, number).wait_send())
             owned(j, p, lambda: all_wait(s, j, many * plan_count - 1).wait_send())
@@ -669,10 +714,12 @@
         for copy in copies:
             copy.wait_recv()
 
-    pile_terms(0)
+    start(init[0:2])
     start_parts(0)
+    start(init[2:])
     arrive(init[0:2])
     start_numbers()
+    middle_parts(0)
     arrive(init[2:4])
     cell_terms(0)
     arrive(init[4:])
@@ -682,15 +729,19 @@
     pile_terms(1)
     start_parts(1)
     update_pile(0)
+    middle_parts(1)
+    own_pile(0)
     arrive(halos[0])
     new_stress(0)
+    update_pile(1)
     wait_pile(0)
     cell_terms(1)
-    update_pile(1)
     new_velocity(1)
     halos.append(start(halo_leg(1)))
     pile_terms(2)
     start_parts(2)
+    own_pile(1)
+    middle_parts(2)
     arrive(halos[1])
     new_stress(1)
     wait_pile(1)
@@ -748,7 +799,7 @@
     width = pile_mass.shape[0]
     tiles = width // 1024
     pairs = pair_elem.shape[1]
-    chunk = min(512, pairs)
+    chunk = min(1024, pairs)
     units = 3 * tiles
     slots = -(-units // plan_count)
     rows = cz * cx
@@ -791,6 +842,8 @@
         vm(3 * rows, cy),
         vm(rows, cy),
         vm(STEPS, 3, units, 8, 128),
+        vm(STEPS, 2, units, 8, 128),
+        vm(STEPS, units, 8, 128),
         vm(STEPS, slots, 3 * plan_count, 8, 128),
         vm(3, tiles, 8, 128),
         vm(2, tiles, 8, 128),
@@ -810,6 +863,10 @@
         dma(slots),
         dma(STEPS, slots),
         dma(STEPS, slots),
+        dma(STEPS, 2),
+        dma(STEPS, 2),
+        dma(STEPS, 2),
+        dma(STEPS, 2),
     ]
     anywhere = pl.BlockSpec(memory_space=pl.ANY)
     stress, velocity, pile = pl.pallas_call(

time: 89.6 us -> 75.9 us (0.85)
  Pallas kernels: 85 us -> 71.3 us
    pallas_call x1, Pallas kernels: 85 us -> 71.3 us  [shards(): pl.pallas_call(functools.partial(kernel, sizes), out_shape=(jax.ShapeDtyp...]
where the time goes in v3:
time: 75.9 us; the launch traced here: 75.7 us
  Pallas kernels  71.3 us (94%)
  local copies, waits for them, and re-layouts  3.75 us (5%)
    pallas_call x1, Pallas kernels, shards(): pl.pallas_call(functools.partial(kernel, sizes), out_shape=(jax.ShapeDtyp...  71.3 us
    unnamed x7, local copies, waits for them, and re-layouts  3.75 us

profile of v3, /device:TPU:8, one launch (start us, length us, event | category | flops | bytes accessed | tf_op | source)
XLA Modules:
  0.0 75.7 jit_solution(14000846763703996268)
XLA Ops:
  0.6 71.3 %shard_map.112 = (f32[6,8,16,256]{3,2,1,0:T(8,128)}, f32[3,8,16,256]{3,2,1,0:T(8,128)}, f32[3,6144]{1,0:T(4,128)}) custom-call(f32[6,8,16,256]{3,2,1,0:T(8,128)} %stress.1, f32[3,8,16,256]{3,2,1,0:T(8,128)} %velocity.1, f32[8,16,256]{2,1,0:T(8,128)} %density.1, s32[8,16,256]{2,1,0:T(8,128)} %flags.1, f32[3,6144]{1,0:T(4,128)} %pile0.1, ...), custom_call_target="tpu_custom_call" | custom-call | tf_op jit(solution)/shard_map/pallas_call | solution.py:872
  71.9 0.0 copy-start
  71.9 2.1 %copy.15 = f32[6,8,16,256]{3,2,1,0:T(8,128)} copy(f32[6,8,16,256]{3,2,1,0:T(8,128)} %get-tuple-element.6) | data formatting | bytes 1572864
  74.1 0.0 copy-done
  74.1 0.0 copy-start.1
  74.1 0.7 copy.16
  74.8 0.2 copy-done.1
  75.1 0.6 copy.17
Async XLA Ops:
  71.9 2.2 %copy-start = (f32[3,8,16,256]{3,2,1,0:T(8,128)S(1)}, f32[3,8,16,256]{3,2,1,0:T(8,128)}, u32[]{:S(2)}) copy-start(f32[3,8,16,256]{3,2,1,0:T(8,128)} %get-tuple-element.7) | copy-start | bytes 1179652
  74.1 1.0 %copy-start.1 = (f32[3,6144]{1,0:T(4,128)S(1)}, f32[3,6144]{1,0:T(4,128)}, u32[]{:S(2)}) copy-start(f32[3,6144]{1,0:T(4,128)} %get-tuple-element.8) | copy-start | bytes 221188

commit v4 on v3

--- a/solution.py
+++ b/solution.py
@@ -202,7 +202,9 @@
             barrier, inc=1, device_id={"depth": dd, "plan": q}, device_id_type=MESH
         )
 
-    everyone(0, greet)
+    everyone(2, greet)
+    for dd, pp in ((d_dn, p), (d_up, p)) + corners:
+        greet(0, dd, 1, pp)
     for i in (0, 3):
         local[i].wait()
 
@@ -335,7 +337,7 @@
             nbuf[b, t] = acc_s[r : r + 8, l : l + 128]
     phi[...] = jnp.zeros_like(phi)
     pile_terms(0)
-    pl.semaphore_wait(barrier, 3 * plan_count - 1)
+    pl.semaphore_wait(barrier, plan_count + 5)
     mine = pl.ds(units, units)
     init = [
         remote(
@@ -577,7 +579,11 @@
         xs1 = pl.ds(2 - w, w)
         mid = pl.ds(8, cz)
         send = lambda i: (halo_send.at[s, i], halo_recv.at[s, i])
-        copies = [
+        copies = []
+        if s < STEPS - 1:
+            for i in range(4):
+                copies.append(remote(cbuf.at[s, i], crx.at[s, i], *send(4 + i), *corners[i]))
+        copies += [
             remote(
                 vx.at[s, :, pl.ds(cz + 2 - w, w), own, :],
                 vx.at[s, :, pl.ds(2 - w, w), own, :],
@@ -595,9 +601,6 @@
             remote(pbuf.at[s, 0, :, xs0], rxp.at[s, 1, :, xs0, mid, :], *send(2), d, p_dn),
             remote(pbuf.at[s, 1, :, xs1], rxp.at[s, 0, :, xs1, mid, :], *send(3), d, p_up),
         ]
-        if s < STEPS - 1:
-            for i in range(4):
-                copies.append(remote(cbuf.at[s, i], crx.at[s, i], *send(4 + i), *corners[i]))
         return copies
 
     def new_stress(s):

time: 75.9 us -> 74.7 us (0.984)
  Pallas kernels: 71.3 us -> 70.1 us
    pallas_call x1, Pallas kernels: 71.3 us -> 70.1 us  [shards(): pl.pallas_call(functools.partial(kernel, sizes), out_shape=(jax.ShapeDtyp...]
where the time goes in v4:
time: 74.7 us; the launch traced here: 74.5 us
  Pallas kernels  70.1 us (94%)
  local copies, waits for them, and re-layouts  3.75 us (5%)
    pallas_call x1, Pallas kernels, shards(): pl.pallas_call(functools.partial(kernel, sizes), out_shape=(jax.ShapeDtyp...  70.1 us
    unnamed x7, local copies, waits for them, and re-layouts  3.75 us

profile of v4, /device:TPU:8, one launch (start us, length us, event | category | flops | bytes accessed | tf_op | source)
XLA Modules:
  0.0 74.5 jit_solution(14802959354700259490)
XLA Ops:
  0.6 70.1 %shard_map.112 = (f32[6,8,16,256]{3,2,1,0:T(8,128)}, f32[3,8,16,256]{3,2,1,0:T(8,128)}, f32[3,6144]{1,0:T(4,128)}) custom-call(f32[6,8,16,256]{3,2,1,0:T(8,128)} %stress.1, f32[3,8,16,256]{3,2,1,0:T(8,128)} %velocity.1, f32[8,16,256]{2,1,0:T(8,128)} %density.1, s32[8,16,256]{2,1,0:T(8,128)} %flags.1, f32[3,6144]{1,0:T(4,128)} %pile0.1, ...), custom_call_target="tpu_custom_call" | custom-call | tf_op jit(solution)/shard_map/pallas_call | solution.py:875
  70.7 0.0 copy-start
  70.7 2.1 %copy.15 = f32[6,8,16,256]{3,2,1,0:T(8,128)} copy(f32[6,8,16,256]{3,2,1,0:T(8,128)} %get-tuple-element.6) | data formatting | bytes 1572864
  72.8 0.0 copy-done
  72.9 0.0 copy-start.1
  72.9 0.7 %copy.16 = f32[3,8,16,256]{3,2,1,0:T(8,128)} copy(f32[3,8,16,256]{3,2,1,0:T(8,128)S(1)} %copy-done) | data formatting | bytes 786432
  73.6 0.2 copy-done.1
  73.8 0.6 copy.17
Async XLA Ops:
  70.7 2.2 %copy-start = (f32[3,8,16,256]{3,2,1,0:T(8,128)S(1)}, f32[3,8,16,256]{3,2,1,0:T(8,128)}, u32[]{:S(2)}) copy-start(f32[3,8,16,256]{3,2,1,0:T(8,128)} %get-tuple-element.7) | copy-start | bytes 1179652
  72.9 1.0 %copy-start.1 = (f32[3,6144]{1,0:T(4,128)S(1)}, f32[3,6144]{1,0:T(4,128)}, u32[]{:S(2)}) copy-start(f32[3,6144]{1,0:T(4,128)} %get-tuple-element.8) | copy-start | bytes 221188

commit v5 on v4

--- a/solution.py
+++ b/solution.py
@@ -565,7 +565,7 @@
                     pbuf[s, 1, c, 0, row, :] = new[cx - 2 : cx - 1]
             return unused
 
-        lax.fori_loop(0, cz, body, 0)
+        lax.fori_loop(0, cz, body, 0, unroll=2)
         if s < STEPS - 1:
             for i in range(4):
                 z = cz - 1 if i // 2 else 0
@@ -669,9 +669,9 @@
             return unused
 
         if last:
-            lax.fori_loop(1, cz + 1, body, 0)
+            lax.fori_loop(1, cz + 1, body, 0, unroll=2)
             return
-        lax.fori_loop(0, cz + 2, body, 0)
+        lax.fori_loop(0, cz + 2, body, 0, unroll=2)
         for side in range(2):
             inner = [pbuf[s, side, c, side] for c in range(3)]
             outer = [rxp[s, side, c, side, 8 : 8 + cz, :] for c in range(3)]
@@ -721,8 +721,8 @@
     start_parts(0)
     start(init[2:])
     arrive(init[0:2])
+    middle_parts(0)
     start_numbers()
-    middle_parts(0)
     arrive(init[2:4])
     cell_terms(0)
     arrive(init[4:])

time: 74.7 us -> 74.6 us (level)
  no operation moved by 1% of the time
where the time goes in v5:
time: 74.6 us; the launch traced here: 74.4 us
  Pallas kernels  70 us (94%)
  local copies, waits for them, and re-layouts  3.75 us (5%)
    pallas_call x1, Pallas kernels, shards(): pl.pallas_call(functools.partial(kernel, sizes), out_shape=(jax.ShapeDtyp...  70 us
    unnamed x7, local copies, waits for them, and re-layouts  3.75 us

profile of v5, /device:TPU:8, one launch (start us, length us, event | category | flops | bytes accessed | tf_op | source)
XLA Modules:
  0.0 74.4 jit_solution(15567838510384811895)
XLA Ops:
  0.6 70.0 %shard_map.112 = (f32[6,8,16,256]{3,2,1,0:T(8,128)}, f32[3,8,16,256]{3,2,1,0:T(8,128)}, f32[3,6144]{1,0:T(4,128)}) custom-call(f32[6,8,16,256]{3,2,1,0:T(8,128)} %stress.1, f32[3,8,16,256]{3,2,1,0:T(8,128)} %velocity.1, f32[8,16,256]{2,1,0:T(8,128)} %density.1, s32[8,16,256]{2,1,0:T(8,128)} %flags.1, f32[3,6144]{1,0:T(4,128)} %pile0.1, ...), custom_call_target="tpu_custom_call" | custom-call | tf_op jit(solution)/shard_map/pallas_call | solution.py:875
  70.6 0.0 copy-start
  70.6 2.1 %copy.15 = f32[6,8,16,256]{3,2,1,0:T(8,128)} copy(f32[6,8,16,256]{3,2,1,0:T(8,128)} %get-tuple-element.6) | data formatting | bytes 1572864
  72.8 0.0 copy-done
  72.8 0.0 copy-start.1
  72.8 0.7 %copy.16 = f32[3,8,16,256]{3,2,1,0:T(8,128)} copy(f32[3,8,16,256]{3,2,1,0:T(8,128)S(1)} %copy-done) | data formatting | bytes 786432
  73.5 0.2 copy-done.1
  73.8 0.6 copy.17
Async XLA Ops:
  70.6 2.2 %copy-start = (f32[3,8,16,256]{3,2,1,0:T(8,128)S(1)}, f32[3,8,16,256]{3,2,1,0:T(8,128)}, u32[]{:S(2)}) copy-start(f32[3,8,16,256]{3,2,1,0:T(8,128)} %get-tuple-element.7) | copy-start | bytes 1179652
  72.8 1.0 %copy-start.1 = (f32[3,6144]{1,0:T(4,128)S(1)}, f32[3,6144]{1,0:T(4,128)}, u32[]{:S(2)}) copy-start(f32[3,6144]{1,0:T(4,128)} %get-tuple-element.8) | copy-start | bytes 221188
